TPU v7x, 128 devices: a whole 4x4x4 slice. The times are simulated.
128 devices in a mesh: tm: 32 (over x, z, y_hi), head: 4 (over y_lo, core).
Axes of the slice: x: 4, y: 4 (y_hi: 2, y_lo: 2; y = y_hi * 2 + y_lo), z: 4, core: 2. Of those that a mesh axis runs over, the one named last changes fastest.
Arguments:
- query_raw: bfloat16 [16384, 2560], P('tm', 'head'), may hold values from -100 to 100
- key_raw: bfloat16 [16384, 2560], P('tm', 'head'), may hold values from -100 to 100
- values: bfloat16 [16384, 2560], P('tm', 'head'), may hold values from -6 to 6
- query_gain: float32 [2560], P('head'), may hold values from 0.1 to 1.9
- key_gain: float32 [2560], P('head'), may hold values from 0.1 to 1.9
- out_grad: bfloat16 [16384, 2560], P('tm', 'head'), may hold values from -60 to 60
- block_mask: int32 [128, 20], replicated, may hold values 0 or 1
- band_strides: int32 [3], replicated, may hold values from 1 to 16, as said below
Outputs:
- attended: bfloat16 [16384, 2560], P('tm', 'head')
- query_grad: bfloat16 [16384, 2560], P('tm', 'head')
- key_grad: bfloat16 [16384, 2560], P('tm', 'head')
- value_grad: bfloat16 [16384, 2560], P('tm', 'head')
- query_gain_grad: float32 [2560], P('head')
- key_gain_grad: float32 [2560], P('head')
Inputs may be any that keep to these rules, and one draw needn't show every extreme that they name: `band_strides`: entry 0 is 1; every other entry is 2 or more; at least one entry of 1 to 2 is 2 to the power 2 + 2.
All inputs are finite; a program needn't handle non-finite values.
Results may differ from a plain program's by a relative error of at most 0.019.
Values may be sent and summed in bfloat16 or wider, within the bound.
No kernel may reach another device: no remote copies, remote signals or barrier semaphores. Data moves between devices by JAX's collectives and lax.ppermute only.
A program may use at most 128 MiB of HBM per device.

v0:
```python
import functools
import math

import jax
import jax.numpy as jnp
from jax import lax
from jax.experimental import pallas as pl
from jax.experimental.pallas import tpu as pltpu
from jax.sharding import PartitionSpec as P

HEAD_DIM = 128
BLK = 128
WIN = 2
BLOCKS_HERE = 4
TOK = BLK * BLOCKS_HERE
WINDOWS = 6
ROUNDS = 12
NORM_EPSILON = 1e-06
DEAD = -1e30
SCALE = 1.0 / math.sqrt(HEAD_DIM)
LOG2E = math.log2(math.e)
LN2 = math.log(2.0)


def to_near(value, axis):
    return lax.ppermute(value, axis, [(s, s ^ 2) for s in range(lax.axis_size(axis))])


def to_far(value, axis):
    count = lax.axis_size(axis)
    pairs = [(s, s - 2 if s // 2 % 2 == 0 else s + 2) for s in range(count)]
    return lax.ppermute(value, axis, [(s, d) for s, d in pairs if 0 <= d < count])


def swapped(value, axis):
    return lax.ppermute(value, axis, [(s, s ^ 1) for s in range(lax.axis_size(axis))])


def summed_over_groups(value):
    count = lax.axis_size("tm")
    unit = 1
    while unit < count:
        radix = 4 if unit > 1 else 2
        parts = []
        for turn in range(1, radix):
            pairs = []
            for s in range(count):
                digit = s // unit % radix
                pairs.append((s, s + ((digit + turn) % radix - digit) * unit))
            parts.append(lax.ppermute(value, "tm", pairs))
        for part in parts:
            value = value + part
        unit *= radix
    return value


def contract(left, right, left_dim, right_dim):
    return lax.dot_general(
        left, right, (((left_dim,), (right_dim,)), ((), ())), preferred_element_type=jnp.float32
    )


def live_tables(chain_pos, groups, block_mask, band_strides):
    partner = chain_pos ^ 1
    query_groups = jnp.stack([chain_pos, partner])
    near_step = jnp.where(chain_pos // 2 % 2 == 0, 2, -2)
    window_groups = jnp.stack(
        [
            chain_pos,
            partner,
            chain_pos + near_step,
            partner + near_step,
            chain_pos - near_step,
            partner - near_step,
        ]
    )
    apart = window_groups[None, :] - query_groups[:, None]
    inside = (window_groups >= 0) & (window_groups < groups)
    near = (jnp.abs(apart) <= WIN) & inside[None, :]
    pair_first = (chain_pos // 2) * 2 * BLOCKS_HERE
    pair_mask = lax.dynamic_slice_in_dim(block_mask, pair_first, 2 * BLOCKS_HERE, 0)
    pair_mask = pair_mask.reshape(2, BLOCKS_HERE, 2 * WIN + 1, BLOCKS_HERE)
    masks = jnp.where(chain_pos % 2 == 0, pair_mask, pair_mask[::-1])
    levels = jnp.arange(2 * WIN + 1, dtype=jnp.int32) - WIN
    picked = jnp.sum(
        jnp.where(
            apart[:, None, :, None, None] == levels[None, None, None, :, None],
            masks[:, :, None, :, :],
            0,
        ),
        axis=3,
    )
    stride = jnp.sum(
        jnp.where(
            jnp.abs(apart)[:, :, None] == jnp.arange(WIN + 1, dtype=jnp.int32),
            band_strides,
            0,
        ),
        axis=2,
    )
    stride = jnp.maximum(stride, 1)
    within = jnp.arange(BLOCKS_HERE, dtype=jnp.int32)
    query_block = query_groups[:, None] * BLOCKS_HERE + within[None, :]
    key_block = window_groups[:, None] * BLOCKS_HERE + within[None, :]
    total = query_block[:, :, None, None] + key_block[None, None, :, :]
    hit = total % stride[:, None, :, None] == 0
    aligned = within[:, None] == within[None, :]
    live = ((picked == 1) & hit | aligned[None, :, None, :]) & near[:, None, :, None]
    centre = jnp.stack([live[0, :, 0, :], live[1, :, 1, :]])
    slots = jnp.arange(WINDOWS, dtype=jnp.int32)
    is_centre = slots[None, :] == jnp.arange(2, dtype=jnp.int32)[:, None]
    scattered = live & ~aligned[None, :, None, :] & ~is_centre[:, None, :, None]
    scattered = scattered.reshape(2, BLOCKS_HERE, WINDOWS * BLOCKS_HERE)
    rank = jnp.cumsum(scattered.astype(jnp.int32), axis=2) - 1
    rounds = jnp.arange(ROUNDS, dtype=jnp.int32)
    chosen = scattered[:, None] & (rank[:, None] == rounds[None, :, None, None])
    places = jnp.arange(WINDOWS * BLOCKS_HERE, dtype=jnp.int32)
    place = jnp.sum(jnp.where(chosen, places, 0), axis=3)
    used = jnp.any(chosen, axis=3)
    count = jnp.max(jnp.sum(scattered.astype(jnp.int32), axis=2), axis=1)
    same = (chain_pos // 2 % 2 == chain_pos % 2).astype(jnp.int32)
    offs = jnp.stack(
        [
            jnp.stack([jnp.int32(1), jnp.int32(2), jnp.int32(4), 3 + 2 * same]),
            jnp.stack([jnp.int32(0), jnp.int32(3), jnp.int32(5), 4 - 2 * same]),
        ]
    )
    off_inside = jnp.sum(
        jnp.where(offs[:, :, None] == slots[None, None, :], near[:, None, :].astype(jnp.int32), 0),
        axis=2,
    )
    ints = jnp.concatenate([place.reshape(2, -1), offs, count[:, None]], axis=1)
    flags = jnp.concatenate(
        [used.reshape(2, -1), centre.reshape(2, -1), off_inside == 1], axis=1
    )
    return ints, jnp.where(flags, 0.0, DEAD).astype(jnp.float32)


INT_OFFS = ROUNDS * BLOCKS_HERE
INT_COUNT = INT_OFFS + 4
BIAS_CENTRE = ROUNDS * BLOCKS_HERE
BIAS_OFF = BIAS_CENTRE + 16


def fold_rows(tile, op):
    return op(tile.reshape(BLK // 8, 8, BLK), axis=0)


def attention_kernel(
    groups_here,
    ints,
    bias,
    query,
    grad,
    own,
    partner,
    near_own,
    near_partner,
    far_own,
    far_partner,
    own_rows,
    pair_rows,
    near_back,
    far_back,
    local,
    gains,
    keys,
    keys_t,
    vals,
    vals_t,
    off_keys,
    off_vals,
    off_keys_t,
    off_vals_t,
    grad_keys,
    grad_vals,
    centre_w,
    centre_b,
    centre_d,
    off_w,
    off_b,
    off_d,
    extra_w,
    extra_b,
    out_t,
    top_rows,
    sum_rows,
    grad_scaled,
    gain_rows,
):
    windows = (own, partner, near_own, near_partner, far_own, far_partner)
    for w, ref in enumerate(windows):
        for j in range(BLOCKS_HERE):
            rows = pl.ds(j * BLK, BLK)
            key = ref[0, rows, :]
            value = ref[1, rows, :]
            keys[w * 4 + j] = key
            vals[w * 4 + j] = value
            keys_t[w * 4 + j] = key.T
            vals_t[w * 4 + j] = value.T
    gain_rows[...] = jnp.zeros_like(gain_rows)
    grad_keys[...] = jnp.zeros_like(grad_keys)
    grad_vals[...] = jnp.zeros_like(grad_vals)

    def put_rows(g, kind, i, tile):
        rows = pl.ds(i * BLK, BLK)
        if groups_here == 1:
            own_rows[kind, rows, :] = tile
            return

        @pl.when(g == 0)
        def _():
            own_rows[kind, rows, :] = tile

        @pl.when(g == 1)
        def _():
            pair_rows[kind, rows, :] = tile

    def group_task(g, carry):
        centre = g * 4
        rounds = ints[g, INT_COUNT]
        offs = [ints[g, INT_OFFS + o] * 4 for o in range(4)]

        def rows_of(i):
            return pl.ds(i * BLK, BLK)

        def gather_off(o, c):
            at = ints[g, INT_OFFS + o] * 4
            there = pl.ds(pl.multiple_of(o * BLK, BLK), BLK)
            for i in range(4):
                off_keys[i, there, :] = keys[at + i]
                off_vals[i, there, :] = vals[at + i]
                off_keys_t[i, :, there] = keys_t[at + i]
                off_vals_t[i, :, there] = vals_t[at + i]
            return c

        lax.fori_loop(0, 4, gather_off, 0)

        query_all = query[g]
        query_rows = [query[g, rows_of(i), :] for i in range(4)]
        centre_keys = keys[pl.ds(centre, 4)].reshape(TOK, HEAD_DIM)
        for i in range(4):
            off_w[i] = contract(off_keys[i], query_rows[i], 1, 1)
        centre_w[...] = contract(centre_keys, query_all, 1, 1)
        for i in range(4):
            best = None
            for j in range(4):
                part = fold_rows(centre_w[rows_of(j), rows_of(i)], jnp.max)
                part = part + bias[g, BIAS_CENTRE + i * 4 + j]
                best = part if best is None else jnp.maximum(best, part)
            for o in range(4):
                part = fold_rows(off_w[i, rows_of(o), :], jnp.max) + bias[g, BIAS_OFF + o]
                best = jnp.maximum(best, part)
            top_rows[i] = best

        def extra_scores(r, c):
            for i in range(4):
                scores = contract(keys[ints[g, r * 4 + i]], query_rows[i], 1, 1)
                extra_w[r * 4 + i] = scores
                part = fold_rows(scores, jnp.max) + bias[g, r * 4 + i]
                top_rows[i] = jnp.maximum(top_rows[i], part)
            return c

        lax.fori_loop(0, rounds, extra_scores, 0)
        tops = [jnp.max(top_rows[i], axis=0, keepdims=True) for i in range(4)]

        for i in range(4):
            total = None
            for j in range(4):
                less = tops[i] - bias[g, BIAS_CENTRE + i * 4 + j]
                weight = jnp.exp2(centre_w[rows_of(j), rows_of(i)] - less)
                centre_w[rows_of(j), rows_of(i)] = weight
                centre_b[rows_of(j), rows_of(i)] = weight.astype(jnp.bfloat16)
                part = fold_rows(weight, jnp.sum)
                total = part if total is None else total + part
            for o in range(4):
                less = tops[i] - bias[g, BIAS_OFF + o]
                weight = jnp.exp2(off_w[i, rows_of(o), :] - less)
                off_w[i, rows_of(o), :] = weight
                off_b[i, rows_of(o), :] = weight.astype(jnp.bfloat16)
                total = total + fold_rows(weight, jnp.sum)
            sum_rows[i] = total
        centre_vals_t = jnp.concatenate([vals_t[centre + j] for j in range(4)], axis=1)
        centre_out = contract(centre_vals_t, centre_b[...], 1, 0)
        for i in range(4):
            out_t[i] = centre_out[:, i * BLK : (i + 1) * BLK] + contract(
                off_vals_t[i], off_b[i], 1, 0
            )

        def extra_out(r, c):
            for i in range(4):
                less = tops[i] - bias[g, r * 4 + i]
                weight = jnp.exp2(extra_w[r * 4 + i] - less)
                extra_w[r * 4 + i] = weight
                weight_b = weight.astype(jnp.bfloat16)
                extra_b[r * 4 + i] = weight_b
                sum_rows[i] = sum_rows[i] + fold_rows(weight, jnp.sum)
                out_t[i] = out_t[i] + contract(vals_t[ints[g, r * 4 + i]], weight_b, 1, 0)
            return c

        lax.fori_loop(0, rounds, extra_out, 0)

        dots = []
        for i in range(4):
            inverse = 1.0 / jnp.sum(sum_rows[i], axis=0, keepdims=True)
            head_out = (out_t[i] * inverse).astype(jnp.bfloat16)
            put_rows(g, 0, i, head_out.T)
            grad_t = grad[g, rows_of(i), :].T.astype(jnp.float32) * inverse
            dots.append(jnp.sum(grad_t * head_out.astype(jnp.float32), axis=0, keepdims=True))
            grad_scaled[rows_of(i), :] = grad_t.astype(jnp.bfloat16).T

        grad_rows = [grad_scaled[rows_of(i), :] for i in range(4)]
        centre_vals = vals[pl.ds(centre, 4)].reshape(TOK, HEAD_DIM)
        flow = contract(centre_vals, grad_scaled[...], 1, 1)
        for i in range(4):
            for j in range(4):
                piece = flow[j * BLK : (j + 1) * BLK, i * BLK : (i + 1) * BLK]
                centre_d[rows_of(j), rows_of(i)] = (
                    centre_w[rows_of(j), rows_of(i)] * (piece - dots[i])
                ).astype(jnp.bfloat16)
            off_flow = contract(off_vals[i], grad_rows[i], 1, 1)
            for o in range(4):
                piece = off_flow[o * BLK : (o + 1) * BLK]
                off_d[i, rows_of(o), :] = (off_w[i, rows_of(o), :] * (piece - dots[i])).astype(
                    jnp.bfloat16
                )
        centre_keys_t = jnp.concatenate([keys_t[centre + j] for j in range(4)], axis=1)
        centre_grad = contract(centre_keys_t, centre_d[...], 1, 0)
        for i in range(4):
            out_t[i] = centre_grad[:, i * BLK : (i + 1) * BLK] + contract(
                off_keys_t[i], off_d[i], 1, 0
            )
        place = pl.ds(centre, 4)
        grad_keys[place] = grad_keys[place] + contract(centre_d[...], query_all, 1, 0).reshape(
            4, BLK, HEAD_DIM
        )
        grad_vals[place] = grad_vals[place] + contract(
            centre_b[...], grad_scaled[...], 1, 0
        ).reshape(4, BLK, HEAD_DIM)
        for i in range(4):
            to_keys = contract(off_d[i], query_rows[i], 1, 0)
            to_vals = contract(off_b[i], grad_rows[i], 1, 0)
            for o in range(4):
                at = offs[o] + i
                grad_keys[at] = grad_keys[at] + to_keys[o * BLK : (o + 1) * BLK]
                grad_vals[at] = grad_vals[at] + to_vals[o * BLK : (o + 1) * BLK]

        def extra_grads(r, c):
            for i in range(4):
                at = ints[g, r * 4 + i]
                piece = contract(vals[at], grad_rows[i], 1, 1)
                score_grad = (extra_w[r * 4 + i] * (piece - dots[i])).astype(jnp.bfloat16)
                out_t[i] = out_t[i] + contract(keys_t[at], score_grad, 1, 0)
                grad_keys[at] = grad_keys[at] + contract(score_grad, query_rows[i], 1, 0)
                grad_vals[at] = grad_vals[at] + contract(extra_b[r * 4 + i], grad_rows[i], 1, 0)
            return c

        lax.fori_loop(0, rounds, extra_grads, 0)
        gain_part = gain_rows[...]
        for i in range(4):
            back = (out_t[i] * SCALE).astype(jnp.bfloat16).T
            put_rows(g, 1, i, back)
            gain_part = gain_part + fold_rows(
                back.astype(jnp.float32) * query_rows[i].astype(jnp.float32), jnp.sum
            )
        gain_rows[...] = gain_part
        return carry

    lax.fori_loop(0, groups_here, group_task, 0)
    gain_sum = jnp.zeros((8, HEAD_DIM), jnp.float32)
    for n in range(WINDOWS * BLOCKS_HERE):
        gain_sum = gain_sum + fold_rows(grad_keys[n] * keys[n].astype(jnp.float32), jnp.sum)
    gains[0:1, :] = jnp.sum(gain_rows[...], axis=0, keepdims=True)
    gains[1:2, :] = jnp.sum(gain_sum, axis=0, keepdims=True)
    for n, (window, source, factor) in enumerate(
        ((1, grad_keys, LN2), (1, grad_vals, 1.0), (0, grad_keys, LN2), (0, grad_vals, 1.0))
    ):
        for j in range(BLOCKS_HERE):
            rows = pl.ds(j * BLK, BLK)
            local[n, rows, :] = source[window * 4 + j] * factor
            near_back[n, rows, :] = (source[(window + 2) * 4 + j] * factor).astype(jnp.bfloat16)
            far_back[n, rows, :] = (source[(window + 4) * 4 + j] * factor).astype(jnp.bfloat16)


def attention_slot(slot, place, groups_here, ints, bias, query, grad, windows):
    token_block = pl.BlockSpec((groups_here, TOK, HEAD_DIM), lambda n: (0, 0, place))
    window_block = pl.BlockSpec((2, TOK, HEAD_DIM), lambda n: (0, 0, slot))
    table = pl.BlockSpec(memory_space=pltpu.SMEM)
    out_token = pl.BlockSpec((2, TOK, HEAD_DIM), lambda n: (0, 0, 0))
    out_grads = pl.BlockSpec((4, TOK, HEAD_DIM), lambda n: (0, 0, 0))
    out_gains = pl.BlockSpec((2, HEAD_DIM), lambda n: (0, 0))
    tiles = WINDOWS * BLOCKS_HERE
    tile = (BLK, BLK)
    return pl.pallas_call(
        functools.partial(attention_kernel, groups_here),
        grid=(1,),
        in_specs=[table, table, token_block, token_block]
        + [window_block] * WINDOWS,
        out_specs=[out_token, out_token, out_grads, out_grads, out_grads, out_gains],
        out_shape=[
            jax.ShapeDtypeStruct((2, TOK, HEAD_DIM), jnp.bfloat16),
            jax.ShapeDtypeStruct((2, TOK, HEAD_DIM), jnp.bfloat16),
            jax.ShapeDtypeStruct((4, TOK, HEAD_DIM), jnp.bfloat16),
            jax.ShapeDtypeStruct((4, TOK, HEAD_DIM), jnp.bfloat16),
            jax.ShapeDtypeStruct((4, TOK, HEAD_DIM), jnp.float32),
            jax.ShapeDtypeStruct((2, HEAD_DIM), jnp.float32),
        ],
        scratch_shapes=[
            pltpu.VMEM((tiles,) + tile, jnp.bfloat16),
            pltpu.VMEM((tiles,) + tile, jnp.bfloat16),
            pltpu.VMEM((tiles,) + tile, jnp.bfloat16),
            pltpu.VMEM((tiles,) + tile, jnp.bfloat16),
            pltpu.VMEM((4, TOK, BLK), jnp.bfloat16),
            pltpu.VMEM((4, TOK, BLK), jnp.bfloat16),
            pltpu.VMEM((4, BLK, TOK), jnp.bfloat16),
            pltpu.VMEM((4, BLK, TOK), jnp.bfloat16),
            pltpu.VMEM((tiles,) + tile, jnp.float32),
            pltpu.VMEM((tiles,) + tile, jnp.float32),
            pltpu.VMEM((TOK, TOK), jnp.float32),
            pltpu.VMEM((TOK, TOK), jnp.bfloat16),
            pltpu.VMEM((TOK, TOK), jnp.bfloat16),
            pltpu.VMEM((4, TOK, BLK), jnp.float32),
            pltpu.VMEM((4, TOK, BLK), jnp.bfloat16),
            pltpu.VMEM((4, TOK, BLK), jnp.bfloat16),
            pltpu.VMEM((ROUNDS * 4,) + tile, jnp.float32),
            pltpu.VMEM((ROUNDS * 4,) + tile, jnp.bfloat16),
            pltpu.VMEM((4,) + tile, jnp.float32),
            pltpu.VMEM((4, 8, BLK), jnp.float32),
            pltpu.VMEM((4, 8, BLK), jnp.float32),
            pltpu.VMEM((TOK, HEAD_DIM), jnp.bfloat16),
            pltpu.VMEM((8, HEAD_DIM), jnp.float32),
        ],
        compiler_params=pltpu.CompilerParams(vmem_limit_bytes=40 * 1024 * 1024),
        cost_estimate=pl.CostEstimate(
            flops=groups_here * 40 * 6 * 2 * BLK**3 * 4,
            bytes_accessed=6 * 1024 * 1024,
            transcendentals=groups_here * 40 * BLK * BLK,
        ),
        name="attention_slot",
    )(ints, bias, query, grad, *windows)


def shards(query_raw, key_raw, values, query_gain, key_gain, out_grad, block_mask, band_strides):
    features = query_raw.shape[1]
    groups = lax.axis_size("tm")
    chain_pos = lax.axis_index("tm")
    even = chain_pos % 2 == 0
    all_features = features * lax.axis_size("head")
    half = 2 * HEAD_DIM

    def keep(x):
        return jnp.where(even, x[..., :half], x[..., half : 2 * half])

    def give(x):
        return jnp.where(even, x[..., half : 2 * half], x[..., :half])

    def last(x):
        return x[..., 2 * half :]

    query_float = query_raw.astype(jnp.float32)
    key_float = key_raw.astype(jnp.float32)
    squares = lax.psum(
        jnp.stack(
            [jnp.sum(key_float * key_float, axis=1), jnp.sum(query_float * query_float, axis=1)]
        ),
        "head",
    )
    inverses = lax.rsqrt(squares / all_features + NORM_EPSILON)
    key_inverse = inverses[0][:, None]
    query_inverse = inverses[1][:, None]
    query_unit = query_float * query_inverse
    key_unit = key_float * key_inverse
    key_normed = (key_unit * key_gain[None, :]).astype(jnp.bfloat16)

    key_values = jnp.stack([key_normed, values])
    own_keys = jnp.concatenate([keep(key_values), last(key_values)], axis=2)
    pair_keys = jnp.concatenate([give(key_values), last(key_values)], axis=2)
    partner_keys = swapped(pair_keys, "tm")
    windows = (
        own_keys,
        partner_keys,
        to_near(own_keys, "tm"),
        to_near(partner_keys, "tm"),
        to_far(own_keys, "tm"),
        to_far(partner_keys, "tm"),
    )

    query_scaled = (query_unit * (query_gain * (SCALE * LOG2E))[None, :]).astype(jnp.bfloat16)
    given_query, _ = lax.optimization_barrier(
        (jnp.stack([give(query_scaled), give(out_grad)]), partner_keys)
    )
    given = swapped(given_query, "tm")
    query_pair = jnp.stack([keep(query_scaled), given[0]])
    grad_pair = jnp.stack([keep(out_grad), given[1]])
    query_last = last(query_scaled)[None]
    grad_last = last(out_grad)[None]
    ints, bias = live_tables(chain_pos, groups, block_mask, band_strides)

    def received(result):
        return (to_near(result[2], "tm"), to_far(result[3], "tm"))

    result_last = attention_slot(2, 0, 1, ints, bias, query_last, grad_last, windows)
    received_last = received(result_last)
    result_first = attention_slot(0, 0, 2, ints, bias, query_pair, grad_pair, windows)
    received_first = received(result_first)
    rows_first = swapped(result_first[1], "tm")
    query_gated, received_last = lax.optimization_barrier((query_pair, received_last))
    result_second = attention_slot(1, 1, 2, ints, bias, query_gated, grad_pair, windows)
    received_second = received(result_second)
    rows_second = swapped(result_second[1], "tm")
    gains, rows_second = lax.optimization_barrier(
        ((result_first[5], result_second[5], result_last[5]), rows_second)
    )

    def part_sum(result, pair, start):
        stop = start + 2
        return (
            result[4][start:stop]
            + pair[0][start:stop].astype(jnp.float32)
            + pair[1][start:stop].astype(jnp.float32)
        )

    kept_grads = []
    given_grads = []
    for result, pair in (
        (result_first, received_first),
        (result_second, received_second),
        (result_last, received_last),
    ):
        back = swapped(part_sum(result, pair, 0).astype(jnp.bfloat16), "tm")
        given_grads.append(back.astype(jnp.float32))
        kept_grads.append(part_sum(result, pair, 2))

    def placed(mine, theirs, rest):
        first = jnp.where(even, mine, theirs)
        second = jnp.where(even, theirs, mine)
        return jnp.concatenate([first, second, rest], axis=-1)

    rows = placed(
        jnp.concatenate([result_first[0], result_second[0]], axis=2),
        jnp.concatenate([rows_first, rows_second], axis=2),
        result_last[0],
    )
    attended = rows[0]
    grad_query = rows[1].astype(jnp.float32)
    grads = placed(
        jnp.concatenate([kept_grads[0], kept_grads[1]], axis=2),
        jnp.concatenate([given_grads[0], given_grads[1]], axis=2),
        kept_grads[2] + given_grads[2],
    )
    grad_key = grads[0]
    grad_value = grads[1].astype(jnp.bfloat16)
    query_back = grad_query * query_gain[None, :]
    key_back = grad_key * key_gain[None, :]
    inner = lax.psum(
        jnp.stack([jnp.sum(query_back * query_unit, axis=1), jnp.sum(key_back * key_unit, axis=1)]),
        "head",
    )
    inner = inner / all_features
    query_grad = (query_inverse * (query_back - query_unit * inner[0][:, None])).astype(jnp.bfloat16)
    key_grad = (key_inverse * (key_back - key_unit * inner[1][:, None])).astype(jnp.bfloat16)
    taken = jnp.concatenate([gains[0], gains[1]], axis=1)
    gains = placed(taken, jnp.zeros_like(taken), gains[2])
    gains = gains * jnp.stack([1.0 / (query_gain * (SCALE * LOG2E)), LN2 / key_gain])
    gains = summed_over_groups(gains)
    return (attended, query_grad, key_grad, grad_value, gains[0], gains[1])


def solution(mesh):
    placed = (
        P("tm", "head"),
        P("tm", "head"),
        P("tm", "head"),
        P("head"),
        P("head"),
        P("tm", "head"),
        P(),
        P(),
    )
    return jax.shard_map(
        shards,
        mesh=mesh,
        in_specs=placed,
        out_specs=(
            P("tm", "head"),
            P("tm", "head"),
            P("tm", "head"),
            P("tm", "head"),
            P("head"),
            P("head"),
        ),
        check_vma=False,
    )
```

profile of v0, /device:TPU:0, one launch (start us, length us, event | category | flops | bytes accessed | tf_op | source)
XLA Modules:
  0.0 149.2 jit_solution(7295877704432695923)
XLA Ops:
  0.7 1.4 fusion.13
  2.1 1.3 fusion.19
  3.4 7.1 %psum.14 = f32[2,512]{1,0:T(2,128)S(1)} all-reduce(f32[2,512]{1,0:T(2,128)S(1)} %pad_maximum_fusion.9), channel_id=1, replica_groups=mesh['tm'=32,'head'=4] {'head'}, use_global_device_ids=true, to_apply=%region_10.11 | all-reduce | flops 1024 | bytes 8192 | tf_op jit(solution)/shard_map/psum | solution.py:462
  10.9 1.0 pad_maximum_fusion.3
  11.9 0.7 collective-permute-start.4
  12.6 5.1 %collective-permute-start.2 = (bf16[2,512,384]{2,1,0:T(8,128)(2,1)S(1)}, bf16[2,512,384]{2,1,0:T(8,128)(2,1)S(1)}, u32[]{:S(2)}, u32[]{:S(2)}) collective-permute-start(bf16[2,512,384]{2,1,0:T(8,128)(2,1)S(1)} %get-tuple-element.76.own), channel_id=1, source_target_pairs={{0,8},{4,12},{8,0},{12,4},{16,24},{20,28},{24,16},{28,20},{32,40},... | collective-permute-start | bytes 2359304 | tf_op jit(solution)/shard_map/ppermute | solution.py:26
  17.7 2.9 %collective-permute-start = (bf16[2,512,384]{2,1,0:T(8,128)(2,1)}, bf16[2,512,384]{2,1,0:T(8,128)(2,1)S(1)}, u32[]{:S(2)}, u32[]{:S(2)}) collective-permute-start(bf16[2,512,384]{2,1,0:T(8,128)(2,1)} %get-tuple-element.75), channel_id=1, source_target_pairs={{0,4},{4,0},{8,12},{12,8},{16,20},{20,16},{24,28},{28,24},{32,36},... | collective-permute-start | bytes 2359304 | tf_op jit(solution)/shard_map/ppermute | solution.py:36
  22.7 0.6 convert_reduce_fusion
  24.2 0.5 fusion.27
  25.7 1.8 %select_bitcast_fusion = (bf16[1,512,256]{2,1,0:T(8,128)(2,1)S(1)}, bf16[1,512,256]{2,1,0:T(8,128)(2,1)}) fusion(pred[]{:T(512)S(6)} %eq.182, bf16[512,640]{1,0:T(8,128)(2,1)} %param.13), kind=kLoop, calls=%fused_computation.61 | loop fusion | flops 262144 | bytes 1048577 | tf_op jit(solution)/shard_map/stack | solution.py:494
  28.2 1.3 fusion.8
  29.6 7.2 %collective-permute-done.partner = bf16[2,512,384]{2,1,0:T(8,128)(2,1)S(1)} collective-permute-done((bf16[2,512,384]{2,1,0:T(8,128)(2,1)}, bf16[2,512,384]{2,1,0:T(8,128)(2,1)S(1)}, u32[]{:S(2)}, u32[]{:S(2)}) %collective-permute-start) | collective-permute-done | bytes 786464 | tf_op jit(solution)/shard_map/ppermute | solution.py:36
  36.9 3.2 %collective-permute-start.1 = (bf16[2,512,256]{2,1,0:T(8,128)(2,1)S(1)}, bf16[2,512,256]{2,1,0:T(8,128)(2,1)S(1)}, u32[]{:S(2)}, u32[]{:S(2)}) collective-permute-start(bf16[2,512,256]{2,1,0:T(8,128)(2,1)S(1)} %pad_maximum_fusion.5), channel_id=1, source_target_pairs={{0,4},{4,0},{8,12},{12,8},{16,20},{20,16},{24,28},{28,24},{32,36},... | collective-permute-start | bytes 1572872 | tf_op jit(solution)/shard_map/ppermute | solution.py:36
  40.1 0.7 collective-permute-start.5
  40.8 3.2 %collective-permute-start.3 = (bf16[2,512,384]{2,1,0:T(8,128)(2,1)S(1)}, bf16[2,512,384]{2,1,0:T(8,128)(2,1)S(1)}, u32[]{:S(2)}, u32[]{:S(2)}) collective-permute-start(bf16[2,512,384]{2,1,0:T(8,128)(2,1)S(1)} %collective-permute-done.partner), channel_id=1, source_target_pairs={{0,8},{4,12},{8,0},{12,4},{16,24},{20,28},{24,16},{28,20},{32,40},... | collective-permute-start | bytes 2359304 | tf_op jit(solution)/shard_map/ppermute | solution.py:26
  44.1 0.9 slice_bitcast_fusion.3
  45.0 4.5 %collective-permute-done.1 = bf16[2,512,256]{2,1,0:T(8,128)(2,1)S(1)} collective-permute-done((bf16[2,512,256]{2,1,0:T(8,128)(2,1)S(1)}, bf16[2,512,256]{2,1,0:T(8,128)(2,1)S(1)}, u32[]{:S(2)}, u32[]{:S(2)}) %collective-permute-start.1) | collective-permute-done | bytes 524320 | tf_op jit(solution)/shard_map/ppermute | solution.py:36
  49.7 8.9 %collective-permute-done.3.near_partner = bf16[2,512,384]{2,1,0:T(8,128)(2,1)S(1)} collective-permute-done((bf16[2,512,384]{2,1,0:T(8,128)(2,1)S(1)}, bf16[2,512,384]{2,1,0:T(8,128)(2,1)S(1)}, u32[]{:S(2)}, u32[]{:S(2)}) %collective-permute-start.3) | collective-permute-done | bytes 786464 | tf_op jit(solution)/shard_map/ppermute | solution.py:26
  58.7 4.7 %attention_slot.4 = (bf16[2,512,128]{2,1,0:T(8,128)(2,1)S(1)}, bf16[2,512,128]{2,1,0:T(8,128)(2,1)}, bf16[4,512,128]{2,1,0:T(8,128)(2,1)S(1)}, bf16[4,512,128]{2...) custom-call(s32[2,53]{1,0:T(2,128)S(1)} %pad_add_fusion.1.ints, ...), custom_call_target="tpu_custom_call" | custom-call | flops 4026531840 | bytes 6291456 | tf_op jit(solution)/shard_map/attention_slot/pallas_call | solution.py:394
  63.4 3.0 %collective-permute-start.6 = (bf16[4,512,128]{2,1,0:T(8,128)(2,1)S(1)}, bf16[4,512,128]{2,1,0:T(8,128)(2,1)S(1)}, u32[]{:S(2)}, u32[]{:S(2)}) collective-permute-start(bf16[4,512,128]{2,1,0:T(8,128)(2,1)S(1)} %get-tuple-element.33), channel_id=1, source_target_pairs={{0,8},{4,12},{8,0},{12,4},{16,24},{20,28},{24,16},{28,20},{32,40},... | collective-permute-start | bytes 1572872 | tf_op jit(solution)/shard_map/ppermute | solution.py:26
  66.5 0.9 collective-permute-start.7
  67.3 10.0 %attention_slot.3 = (bf16[2,512,128]{2,1,0:T(8,128)(2,1)S(1)}, bf16[2,512,128]{2,1,0:T(8,128)(2,1)S(1)}, bf16[4,512,128]{2,1,0:T(8,128)(2,1)S(1)}, bf16[4,512,12...) custom-call(s32[2,53]{1,0:T(2,128)S(1)} %pad_add_fusion.1.ints, ...), custom_call_target="tpu_custom_call" | custom-call | flops 8053063680 | bytes 6291456 | tf_op jit(solution)/shard_map/attention_slot/pallas_call | solution.py:394
  77.5 5.9 %collective-permute-start.10 = (bf16[4,512,128]{2,1,0:T(8,128)(2,1)S(1)}, bf16[4,512,128]{2,1,0:T(8,128)(2,1)S(1)}, u32[]{:S(2)}, u32[]{:S(2)}) collective-permute-start(bf16[4,512,128]{2,1,0:T(8,128)(2,1)S(1)} %get-tuple-element.45), channel_id=1, source_target_pairs={{0,8},{4,12},{8,0},{12,4},{16,24},{20,28},{24,16},{28,20},{32,40},... | collective-permute-start | bytes 1572872 | tf_op jit(solution)/shard_map/ppermute | solution.py:26
  83.3 0.7 collective-permute-start.11
  84.1 2.2 %collective-permute-done.8 = bf16[2,512,128]{2,1,0:T(8,128)(2,1)S(1)} collective-permute-done((bf16[2,512,128]{2,1,0:T(8,128)(2,1)S(1)}, bf16[2,512,128]{2,1,0:T(8,128)(2,1)S(1)}, u32[]{:S(2)}, u32[]{:S(2)}) %collective-permute-start.8) | collective-permute-done | bytes 262176 | tf_op jit(solution)/shard_map/ppermute | solution.py:36
  86.5 10.0 %attention_slot.5 = (bf16[2,512,128]{2,1,0:T(8,128)(2,1)S(1)}, bf16[2,512,128]{2,1,0:T(8,128)(2,1)S(1)}, bf16[4,512,128]{2,1,0:T(8,128)(2,1)S(1)}, bf16[4,512,12...) custom-call(s32[2,53]{1,0:T(2,128)S(1)} %pad_add_fusion.1.ints, ...), custom_call_target="tpu_custom_call" | custom-call | flops 8053063680 | bytes 6291456 | tf_op jit(solution)/shard_map/attention_slot/pallas_call | solution.py:394
  96.5 3.6 %collective-permute-start.9 = (bf16[2,512,128]{2,1,0:T(8,128)(2,1)S(1)}, bf16[2,512,128]{2,1,0:T(8,128)(2,1)S(1)}, u32[]{:S(2)}, u32[]{:S(2)}) collective-permute-start(bf16[2,512,128]{2,1,0:T(8,128)(2,1)S(1)} %get-tuple-element.41), channel_id=1, source_target_pairs={{0,4},{4,0},{8,12},{12,8},{16,20},{20,16},{24,28},{28,24},{32,36},... | collective-permute-start | bytes 786440 | tf_op jit(solution)/shard_map/ppermute | solution.py:36
  100.1 4.3 %collective-permute-start.12 = (bf16[4,512,128]{2,1,0:T(8,128)(2,1)S(1)}, bf16[4,512,128]{2,1,0:T(8,128)(2,1)S(1)}, u32[]{:S(2)}, u32[]{:S(2)}) collective-permute-start(bf16[4,512,128]{2,1,0:T(8,128)(2,1)S(1)} %get-tuple-element.48), channel_id=1, source_target_pairs={{0,8},{4,12},{8,0},{12,4},{16,24},{20,28},{24,16},{28,20},{32,40},... | collective-permute-start | bytes 1572872 | tf_op jit(solution)/shard_map/ppermute | solution.py:26
  104.5 0.7 collective-permute-start.13
  105.4 2.9 %collective-permute-start.17 = (f32[2,640]{1,0:T(2,128)S(1)}, f32[2,640]{1,0:T(2,128)S(1)}, u32[]{:S(2)}, u32[]{:S(2)}) collective-permute-start(f32[2,640]{1,0:T(2,128)S(1)} %maximum_multiply_fusion), channel_id=1, source_target_pairs={{0,4},{4,0},{8,12},{12,8},{16,20},{20,16},{24,28},{28,24},{32,36},... | collective-permute-start | bytes 15368 | tf_op jit(solution)/shard_map/ppermute | solution.py:50
  108.7 0.9 slice_bitcast_fusion.2
  109.6 1.2 collective-permute-done.17
  110.9 8.0 %collective-permute-start.20 = (f32[2,640]{1,0:T(2,128)S(1)}, f32[2,640]{1,0:T(2,128)S(1)}, u32[]{:S(2)}, u32[]{:S(2)}) collective-permute-start(f32[2,640]{1,0:T(2,128)S(1)} %add.239), channel_id=1, source_target_pairs={{0,24},{4,28},{8,0},{12,4},{16,8},{20,12},{24,16},{28,20},{32,56},... | collective-permute-start | bytes 15368 | tf_op jit(solution)/shard_map/ppermute | solution.py:50
  118.8 0.9 collective-permute-start.18
  120.2 1.9 %collective-permute-start.14 = (bf16[2,512,128]{2,1,0:T(8,128)(2,1)S(1)}, bf16[2,512,128]{2,1,0:T(8,128)(2,1)S(1)}, u32[]{:S(2)}, u32[]{:S(2)}) collective-permute-start(bf16[2,512,128]{2,1,0:T(8,128)(2,1)S(1)} %get-tuple-element.69), channel_id=1, source_target_pairs={{0,4},{4,0},{8,12},{12,8},{16,20},{20,16},{24,28},{28,24},{32,36},... | collective-permute-start | bytes 786440 | tf_op jit(solution)/shard_map/ppermute | solution.py:36
  122.1 1.9 %collective-permute-done.19 = f32[2,640]{1,0:T(2,128)S(1)} collective-permute-done((f32[2,640]{1,0:T(2,128)S(1)}, f32[2,640]{1,0:T(2,128)S(1)}, u32[]{:S(2)}, u32[]{:S(2)}) %collective-permute-start.19) | collective-permute-done | bytes 5152 | tf_op jit(solution)/shard_map/ppermute | solution.py:50
  124.0 2.8 %collective-permute-start.23 = (f32[2,640]{1,0:T(2,128)S(1)}, f32[2,640]{1,0:T(2,128)S(1)}, u32[]{:S(2)}, u32[]{:S(2)}) collective-permute-start(f32[2,640]{1,0:T(2,128)S(1)} %add_add_fusion.1), channel_id=1, source_target_pairs={{0,96},{4,100},{8,104},{12,108},{16,112},{20,116},{24,120},{28,124... | collective-permute-start | bytes 15368 | tf_op jit(solution)/shard_map/ppermute | solution.py:50
  126.8 1.5 %collective-permute-start.22 = (f32[2,640]{1,0:T(2,128)S(1)}, f32[2,640]{1,0:T(2,128)S(1)}, u32[]{:S(2)}, u32[]{:S(2)}) collective-permute-start(f32[2,640]{1,0:T(2,128)S(1)} %add_add_fusion.1), channel_id=1, source_target_pairs={{0,64},{4,68},{8,72},{12,76},{16,80},{20,84},{24,88},{28,92},{32,9... | collective-permute-start | bytes 15368 | tf_op jit(solution)/shard_map/ppermute | solution.py:50
  128.3 0.9 collective-permute-start.21
  129.4 2.6 %collective-permute-start.15 = (bf16[2,512,128]{2,1,0:T(8,128)(2,1)S(1)}, bf16[2,512,128]{2,1,0:T(8,128)(2,1)S(1)}, u32[]{:S(2)}, u32[]{:S(2)}) collective-permute-start(bf16[2,512,128]{2,1,0:T(8,128)(2,1)S(1)} %get-tuple-element.71), channel_id=1, source_target_pairs={{0,4},{4,0},{8,12},{12,8},{16,20},{20,16},{24,28},{28,24},{32,36},... | collective-permute-start | bytes 786440 | tf_op jit(solution)/shard_map/ppermute | solution.py:36
  132.0 1.1 collective-permute-done.21
  133.1 0.6 slice_reduce_fusion.2
  133.8 3.6 %collective-permute-done.15 = bf16[2,512,128]{2,1,0:T(8,128)(2,1)S(1)} collective-permute-done((bf16[2,512,128]{2,1,0:T(8,128)(2,1)S(1)}, bf16[2,512,128]{2,1,0:T(8,128)(2,1)S(1)}, u32[]{:S(2)}, u32[]{:S(2)}) %collective-permute-start.15) | collective-permute-done | bytes 262176 | tf_op jit(solution)/shard_map/ppermute | solution.py:36
  137.7 0.9 copy-done.3
  139.0 0.9 fusion.22
  140.0 5.7 %psum.15 = f32[2,512]{1,0:T(2,128)S(1)} all-reduce(f32[2,512]{1,0:T(2,128)S(1)} %pad_maximum_fusion.10), channel_id=1, replica_groups=mesh['tm'=32,'head'=4] {'head'}, use_global_device_ids=true, to_apply=%region_13.14 | all-reduce | flops 1024 | bytes 8192 | tf_op jit(solution)/shard_map/psum | solution.py:555
  145.6 2.4 %fusion.12 = bf16[512,640]{1,0:T(8,128)(2,1)} fusion(bf16[512,640]{1,0:T(8,128)(2,1)S(1)} %copy-done.1, f32[512]{0:T(512)S(1)} %bitcast.77, f32[640]{0:T(1024)S(1)} %copy-done.9, f32[512]{0:T(512)S(1)} %bitcast.72, bf16[2,512,640]{2,1,0:T(8,128)(2,1)} %copy-done.5), kind=kLoop, calls=%fused_computation.24 | loop fusion | flops 2621440 | bytes 1972736 | tf_op jit(solution)/shard_map/convert_element_type | solution.py:560
  148.0 1.2 fusion.18
  (131 shorter events, 7.7 us)
Async XLA Ops:
  0.6 21.4 %copy-start = (s32[128,20]{0,1:T(8,128)S(1)}, s32[128,20]{0,1:T(8,128)}, u32[]{:S(2)}) copy-start(s32[128,20]{0,1:T(8,128)} %param.14) | copy-start | bytes 30724
  0.6 9.8 %copy-start.2 = (bf16[512,640]{1,0:T(8,128)(2,1)S(1)}, bf16[512,640]{1,0:T(8,128)(2,1)}, u32[]{:S(2)}) copy-start(bf16[512,640]{1,0:T(8,128)(2,1)} %param.9) | copy-start | bytes 1966084
  0.7 9.8 %copy-start.8 = (f32[640]{0:T(1024)S(1)}, f32[640]{0:T(1024)}, u32[]{:S(2)}) copy-start(f32[640]{0:T(1024)} %param.12) | copy-start | bytes 7684
  0.7 10.0 %copy-start.6 = (bf16[512,640]{1,0:T(8,128)(2,1)S(1)}, bf16[512,640]{1,0:T(8,128)(2,1)}, u32[]{:S(2)}) copy-start(bf16[512,640]{1,0:T(8,128)(2,1)} %param.10) | copy-start | bytes 1966084
  10.8 10.2 %copy-start.10 = (s32[3]{0:T(128)S(1)}, s32[3]{0:T(128)}, u32[]{:S(2)}) copy-start(s32[3]{0:T(128)} %param.15) | copy-start | bytes 40
  10.9 14.3 %copy-start.9 = (f32[640]{0:T(1024)S(1)}, f32[640]{0:T(1024)}, u32[]{:S(2)}) copy-start(f32[640]{0:T(1024)} %param.11) | copy-start | bytes 7684
  11.9 37.8 %collective-permute-start.4 = (bf16[2,512,384]{2,1,0:T(8,128)(2,1)S(1)}, bf16[2,512,384]{2,1,0:T(8,128)(2,1)S(1)}, u32[]{:S(2)}, u32[]{:S(2)}) collective-permute-start(bf16[2,512,384]{2,1,0:T(8,128)(2,1)S(1)} %get-tuple-element.76.own), channel_id=1, source_target_pairs={{8,16},{12,20},{16,8},{20,12},{24,32},{28,36},{32,24},{36,28},{40,... | collective-permute-start | bytes 2359304 | tf_op jit(solution)/shard_map/ppermute | solution.py:32
  12.6 37.1 %collective-permute-start.2 = (bf16[2,512,384]{2,1,0:T(8,128)(2,1)S(1)}, bf16[2,512,384]{2,1,0:T(8,128)(2,1)S(1)}, u32[]{:S(2)}, u32[]{:S(2)}) collective-permute-start(bf16[2,512,384]{2,1,0:T(8,128)(2,1)S(1)} %get-tuple-element.76.own), channel_id=1, source_target_pairs={{0,8},{4,12},{8,0},{12,4},{16,24},{20,28},{24,16},{28,20},{32,40},... | collective-permute-start | bytes 2359304 | tf_op jit(solution)/shard_map/ppermute | solution.py:26
  17.7 19.1 %collective-permute-start = (bf16[2,512,384]{2,1,0:T(8,128)(2,1)}, bf16[2,512,384]{2,1,0:T(8,128)(2,1)S(1)}, u32[]{:S(2)}, u32[]{:S(2)}) collective-permute-start(bf16[2,512,384]{2,1,0:T(8,128)(2,1)} %get-tuple-element.75), channel_id=1, source_target_pairs={{0,4},{4,0},{8,12},{12,8},{16,20},{20,16},{24,28},{28,24},{32,36},... | collective-permute-start | bytes 2359304 | tf_op jit(solution)/shard_map/ppermute | solution.py:36
  28.0 1.6 %copy-start.7 = (bf16[1,512,256]{2,1,0:T(8,128)(2,1)S(1)}, bf16[1,512,256]{2,1,0:T(8,128)(2,1)}, u32[]{:S(2)}) copy-start(bf16[1,512,256]{2,1,0:T(8,128)(2,1)} %get-tuple-element.82) | copy-start | bytes 786436
  36.9 12.7 %collective-permute-start.1 = (bf16[2,512,256]{2,1,0:T(8,128)(2,1)S(1)}, bf16[2,512,256]{2,1,0:T(8,128)(2,1)S(1)}, u32[]{:S(2)}, u32[]{:S(2)}) collective-permute-start(bf16[2,512,256]{2,1,0:T(8,128)(2,1)S(1)} %pad_maximum_fusion.5), channel_id=1, source_target_pairs={{0,4},{4,0},{8,12},{12,8},{16,20},{20,16},{24,28},{28,24},{32,36},... | collective-permute-start | bytes 1572872 | tf_op jit(solution)/shard_map/ppermute | solution.py:36
  40.1 9.6 %collective-permute-start.5 = (bf16[2,512,384]{2,1,0:T(8,128)(2,1)S(1)}, bf16[2,512,384]{2,1,0:T(8,128)(2,1)S(1)}, u32[]{:S(2)}, u32[]{:S(2)}) collective-permute-start(bf16[2,512,384]{2,1,0:T(8,128)(2,1)S(1)} %collective-permute-done.partner), channel_id=1, source_target_pairs={{8,16},{12,20},{16,8},{20,12},{24,32},{28,36},{32,24},{36,28},{40,... | collective-permute-start | bytes 2359304 | tf_op jit(solution)/shard_map/ppermute | solution.py:32
  40.8 17.9 %collective-permute-start.3 = (bf16[2,512,384]{2,1,0:T(8,128)(2,1)S(1)}, bf16[2,512,384]{2,1,0:T(8,128)(2,1)S(1)}, u32[]{:S(2)}, u32[]{:S(2)}) collective-permute-start(bf16[2,512,384]{2,1,0:T(8,128)(2,1)S(1)} %collective-permute-done.partner), channel_id=1, source_target_pairs={{0,8},{4,12},{8,0},{12,4},{16,24},{20,28},{24,16},{28,20},{32,40},... | collective-permute-start | bytes 2359304 | tf_op jit(solution)/shard_map/ppermute | solution.py:26
  63.4 22.9 %collective-permute-start.6 = (bf16[4,512,128]{2,1,0:T(8,128)(2,1)S(1)}, bf16[4,512,128]{2,1,0:T(8,128)(2,1)S(1)}, u32[]{:S(2)}, u32[]{:S(2)}) collective-permute-start(bf16[4,512,128]{2,1,0:T(8,128)(2,1)S(1)} %get-tuple-element.33), channel_id=1, source_target_pairs={{0,8},{4,12},{8,0},{12,4},{16,24},{20,28},{24,16},{28,20},{32,40},... | collective-permute-start | bytes 1572872 | tf_op jit(solution)/shard_map/ppermute | solution.py:26
  66.5 19.9 %collective-permute-start.7 = (bf16[4,512,128]{2,1,0:T(8,128)(2,1)S(1)}, bf16[4,512,128]{2,1,0:T(8,128)(2,1)S(1)}, u32[]{:S(2)}, u32[]{:S(2)}) collective-permute-start(bf16[4,512,128]{2,1,0:T(8,128)(2,1)S(1)} %get-tuple-element.34), channel_id=1, source_target_pairs={{8,16},{12,20},{16,8},{20,12},{24,32},{28,36},{32,24},{36,28},{40,... | collective-permute-start | bytes 1572872 | tf_op jit(solution)/shard_map/ppermute | solution.py:32
  77.3 8.9 %collective-permute-start.8 = (bf16[2,512,128]{2,1,0:T(8,128)(2,1)S(1)}, bf16[2,512,128]{2,1,0:T(8,128)(2,1)S(1)}, u32[]{:S(2)}, u32[]{:S(2)}) collective-permute-start(bf16[2,512,128]{2,1,0:T(8,128)(2,1)S(1)} %get-tuple-element.37), channel_id=1, source_target_pairs={{0,4},{4,0},{8,12},{12,8},{16,20},{20,16},{24,28},{28,24},{32,36},... | collective-permute-start | bytes 786440 | tf_op jit(solution)/shard_map/ppermute | solution.py:36
  77.5 27.0 %collective-permute-start.10 = (bf16[4,512,128]{2,1,0:T(8,128)(2,1)S(1)}, bf16[4,512,128]{2,1,0:T(8,128)(2,1)S(1)}, u32[]{:S(2)}, u32[]{:S(2)}) collective-permute-start(bf16[4,512,128]{2,1,0:T(8,128)(2,1)S(1)} %get-tuple-element.45), channel_id=1, source_target_pairs={{0,8},{4,12},{8,0},{12,4},{16,24},{20,28},{24,16},{28,20},{32,40},... | collective-permute-start | bytes 1572872 | tf_op jit(solution)/shard_map/ppermute | solution.py:26
  83.3 21.8 %collective-permute-start.11 = (bf16[4,512,128]{2,1,0:T(8,128)(2,1)S(1)}, bf16[4,512,128]{2,1,0:T(8,128)(2,1)S(1)}, u32[]{:S(2)}, u32[]{:S(2)}) collective-permute-start(bf16[4,512,128]{2,1,0:T(8,128)(2,1)S(1)} %get-tuple-element.46), channel_id=1, source_target_pairs={{8,16},{12,20},{16,8},{20,12},{24,32},{28,36},{32,24},{36,28},{40,... | collective-permute-start | bytes 1572872 | tf_op jit(solution)/shard_map/ppermute | solution.py:32
  86.4 22.2 %collective-permute-start.16 = (bf16[2,512,128]{2,1,0:T(8,128)(2,1)S(1)}, bf16[2,512,128]{2,1,0:T(8,128)(2,1)S(1)}, u32[]{:S(2)}, u32[]{:S(2)}) collective-permute-start(bf16[2,512,128]{2,1,0:T(8,128)(2,1)S(1)} %add_convert_fusion), channel_id=1, source_target_pairs={{0,4},{4,0},{8,12},{12,8},{16,20},{20,16},{24,28},{28,24},{32,36},... | collective-permute-start | bytes 786440 | tf_op jit(solution)/shard_map/ppermute | solution.py:36
  96.5 8.8 %collective-permute-start.9 = (bf16[2,512,128]{2,1,0:T(8,128)(2,1)S(1)}, bf16[2,512,128]{2,1,0:T(8,128)(2,1)S(1)}, u32[]{:S(2)}, u32[]{:S(2)}) collective-permute-start(bf16[2,512,128]{2,1,0:T(8,128)(2,1)S(1)} %get-tuple-element.41), channel_id=1, source_target_pairs={{0,4},{4,0},{8,12},{12,8},{16,20},{20,16},{24,28},{28,24},{32,36},... | collective-permute-start | bytes 786440 | tf_op jit(solution)/shard_map/ppermute | solution.py:36
  100.1 28.2 %collective-permute-start.12 = (bf16[4,512,128]{2,1,0:T(8,128)(2,1)S(1)}, bf16[4,512,128]{2,1,0:T(8,128)(2,1)S(1)}, u32[]{:S(2)}, u32[]{:S(2)}) collective-permute-start(bf16[4,512,128]{2,1,0:T(8,128)(2,1)S(1)} %get-tuple-element.48), channel_id=1, source_target_pairs={{0,8},{4,12},{8,0},{12,4},{16,24},{20,28},{24,16},{28,20},{32,40},... | collective-permute-start | bytes 1572872 | tf_op jit(solution)/shard_map/ppermute | solution.py:26
  104.5 24.7 %collective-permute-start.13 = (bf16[4,512,128]{2,1,0:T(8,128)(2,1)S(1)}, bf16[4,512,128]{2,1,0:T(8,128)(2,1)S(1)}, u32[]{:S(2)}, u32[]{:S(2)}) collective-permute-start(bf16[4,512,128]{2,1,0:T(8,128)(2,1)S(1)} %get-tuple-element.49), channel_id=1, source_target_pairs={{8,16},{12,20},{16,8},{20,12},{24,32},{28,36},{32,24},{36,28},{40,... | collective-permute-start | bytes 1572872 | tf_op jit(solution)/shard_map/ppermute | solution.py:32
  105.4 5.4 %collective-permute-start.17 = (f32[2,640]{1,0:T(2,128)S(1)}, f32[2,640]{1,0:T(2,128)S(1)}, u32[]{:S(2)}, u32[]{:S(2)}) collective-permute-start(f32[2,640]{1,0:T(2,128)S(1)} %maximum_multiply_fusion), channel_id=1, source_target_pairs={{0,4},{4,0},{8,12},{12,8},{16,20},{20,16},{24,28},{28,24},{32,36},... | collective-permute-start | bytes 15368 | tf_op jit(solution)/shard_map/ppermute | solution.py:50
  108.6 11.2 %copy-start.5 = (bf16[2,512,640]{2,1,0:T(8,128)(2,1)}, bf16[2,512,640]{2,1,0:T(8,128)(2,1)S(1)}, u32[]{:S(2)}) copy-start(bf16[2,512,640]{2,1,0:T(8,128)(2,1)S(1)} %pad_maximum_fusion.1) | copy-start | bytes 3932164
  108.6 11.2 %copy-start.1 = (bf16[512,640]{1,0:T(8,128)(2,1)S(1)}, bf16[512,640]{1,0:T(8,128)(2,1)}, u32[]{:S(2)}) copy-start(bf16[512,640]{1,0:T(8,128)(2,1)} %param.8) | copy-start | bytes 1966084
  110.9 9.3 %collective-permute-start.20 = (f32[2,640]{1,0:T(2,128)S(1)}, f32[2,640]{1,0:T(2,128)S(1)}, u32[]{:S(2)}, u32[]{:S(2)}) collective-permute-start(f32[2,640]{1,0:T(2,128)S(1)} %add.239), channel_id=1, source_target_pairs={{0,24},{4,28},{8,0},{12,4},{16,8},{20,12},{24,16},{28,20},{32,56},... | collective-permute-start | bytes 15368 | tf_op jit(solution)/shard_map/ppermute | solution.py:50
  118.8 5.1 %collective-permute-start.19 = (f32[2,640]{1,0:T(2,128)S(1)}, f32[2,640]{1,0:T(2,128)S(1)}, u32[]{:S(2)}, u32[]{:S(2)}) collective-permute-start(f32[2,640]{1,0:T(2,128)S(1)} %add.239), channel_id=1, source_target_pairs={{0,16},{4,20},{8,24},{12,28},{16,0},{20,4},{24,8},{28,12},{32,48},... | collective-permute-start | bytes 15368 | tf_op jit(solution)/shard_map/ppermute | solution.py:50
  118.8 5.1 %collective-permute-start.18 = (f32[2,640]{1,0:T(2,128)S(1)}, f32[2,640]{1,0:T(2,128)S(1)}, u32[]{:S(2)}, u32[]{:S(2)}) collective-permute-start(f32[2,640]{1,0:T(2,128)S(1)} %add.239), channel_id=1, source_target_pairs={{0,8},{4,12},{8,16},{12,20},{16,24},{20,28},{24,0},{28,4},{32,40},... | collective-permute-start | bytes 15368 | tf_op jit(solution)/shard_map/ppermute | solution.py:50
  120.2 13.6 %collective-permute-start.14 = (bf16[2,512,128]{2,1,0:T(8,128)(2,1)S(1)}, bf16[2,512,128]{2,1,0:T(8,128)(2,1)S(1)}, u32[]{:S(2)}, u32[]{:S(2)}) collective-permute-start(bf16[2,512,128]{2,1,0:T(8,128)(2,1)S(1)} %get-tuple-element.69), channel_id=1, source_target_pairs={{0,4},{4,0},{8,12},{12,8},{16,20},{20,16},{24,28},{28,24},{32,36},... | collective-permute-start | bytes 786440 | tf_op jit(solution)/shard_map/ppermute | solution.py:36
  124.0 8.0 %collective-permute-start.23 = (f32[2,640]{1,0:T(2,128)S(1)}, f32[2,640]{1,0:T(2,128)S(1)}, u32[]{:S(2)}, u32[]{:S(2)}) collective-permute-start(f32[2,640]{1,0:T(2,128)S(1)} %add_add_fusion.1), channel_id=1, source_target_pairs={{0,96},{4,100},{8,104},{12,108},{16,112},{20,116},{24,120},{28,124... | collective-permute-start | bytes 15368 | tf_op jit(solution)/shard_map/ppermute | solution.py:50
  126.8 5.2 %collective-permute-start.22 = (f32[2,640]{1,0:T(2,128)S(1)}, f32[2,640]{1,0:T(2,128)S(1)}, u32[]{:S(2)}, u32[]{:S(2)}) collective-permute-start(f32[2,640]{1,0:T(2,128)S(1)} %add_add_fusion.1), channel_id=1, source_target_pairs={{0,64},{4,68},{8,72},{12,76},{16,80},{20,84},{24,88},{28,92},{32,9... | collective-permute-start | bytes 15368 | tf_op jit(solution)/shard_map/ppermute | solution.py:50
  128.3 4.8 %collective-permute-start.21 = (f32[2,640]{1,0:T(2,128)S(1)}, f32[2,640]{1,0:T(2,128)S(1)}, u32[]{:S(2)}, u32[]{:S(2)}) collective-permute-start(f32[2,640]{1,0:T(2,128)S(1)} %add_add_fusion.1), channel_id=1, source_target_pairs={{0,32},{4,36},{8,40},{12,44},{16,48},{20,52},{24,56},{28,60},{32,6... | collective-permute-start | bytes 15368 | tf_op jit(solution)/shard_map/ppermute | solution.py:50
  129.4 8.0 %collective-permute-start.15 = (bf16[2,512,128]{2,1,0:T(8,128)(2,1)S(1)}, bf16[2,512,128]{2,1,0:T(8,128)(2,1)S(1)}, u32[]{:S(2)}, u32[]{:S(2)}) collective-permute-start(bf16[2,512,128]{2,1,0:T(8,128)(2,1)S(1)} %get-tuple-element.71), channel_id=1, source_target_pairs={{0,4},{4,0},{8,12},{12,8},{16,20},{20,16},{24,28},{28,24},{32,36},... | collective-permute-start | bytes 786440 | tf_op jit(solution)/shard_map/ppermute | solution.py:36
  137.5 1.1 copy-start.3
  145.6 2.4 %copy-start.4 = (bf16[512,640]{1,0:T(8,128)(2,1)S(1)}, bf16[512,640]{1,0:T(8,128)(2,1)}, u32[]{:S(2)}) copy-start(bf16[512,640]{1,0:T(8,128)(2,1)} %param.9) | copy-start | bytes 1966084
where the time goes:
time: 151 us; the launch traced here: 149 us
  starting transfers between devices  56.5 us (37%)
  waiting for transfers between devices  30.7 us (20%)
  Pallas kernels  24.8 us (16%)
  other arithmetic  16.3 us (11%)
  blocking collectives  12.7 us (8%)
  local copies, waits for them, and re-layouts  6.9 us (5%)
    pallas_call x3, Pallas kernels, attention_slot(): pl.pallas_call(functools.partial(attention_kernel, groups_here), grid=(1,...  24.8 us
    ppermute x5, starting transfers between devices, to_near(): lax.ppermute(value, axis, [(s, s ^ 2) for s in range(lax.axis_size(axis))])  21.5 us
    ppermute x7, waiting for transfers between devices, swapped(): lax.ppermute(value, axis, [(s, s ^ 1) for s in range(lax.axis_size(axis))])  17.5 us
    ppermute x7, starting transfers between devices, summed_over_groups(): parts.append(lax.ppermute(value, 'tm', pairs))  17 us
    ppermute x7, starting transfers between devices, swapped(): lax.ppermute(value, axis, [(s, s ^ 1) for s in range(lax.axis_size(axis))])  14.4 us
    ppermute x5, waiting for transfers between devices, to_near(): lax.ppermute(value, axis, [(s, s ^ 2) for s in range(lax.axis_size(axis))])  8.96 us
    psum x1, blocking collectives, shards(): lax.psum(jnp.stack([jnp.sum(key_float * key_float, axis=1), jnp.sum(query...  7.07 us
    psum x1, blocking collectives, shards(): lax.psum(jnp.stack([jnp.sum(query_back * query_unit, axis=1), jnp.sum(key...  5.66 us
  transfers between devices with their start and end apart: 24, of which 8 were waited for; matrix products, arithmetic and copies ran while one was open for 9% of the time, Pallas kernels for 13%

commit v1 on v0

v1 whole, which is shorter than its diff:
```python
import functools
import math

import jax
import jax.numpy as jnp
from jax import lax
from jax.experimental import pallas as pl
from jax.experimental.pallas import tpu as pltpu
from jax.sharding import PartitionSpec as P

HEAD_DIM = 128
BLK = 128
WIN = 2
BLOCKS_HERE = 4
TOK = BLK * BLOCKS_HERE
WINDOWS = 6
ROUNDS = 12
NORM_EPSILON = 1e-06
DEAD = -1e30
SCALE = 1.0 / math.sqrt(HEAD_DIM)
LOG2E = math.log2(math.e)
LN2 = math.log(2.0)


def to_near(value, axis):
    return lax.ppermute(value, axis, [(s, s ^ 2) for s in range(lax.axis_size(axis))])


def to_far(value, axis):
    count = lax.axis_size(axis)
    pairs = [(s, s - 2 if s // 2 % 2 == 0 else s + 2) for s in range(count)]
    return lax.ppermute(value, axis, [(s, d) for s, d in pairs if 0 <= d < count])


def swapped(value, axis):
    return lax.ppermute(value, axis, [(s, s ^ 1) for s in range(lax.axis_size(axis))])


def summed_over_digit(value, unit, radix):
    parts = []
    for turn in range(1, radix):
        pairs = []
        for s in range(lax.axis_size("tm")):
            digit = s // unit % radix
            pairs.append((s, s + ((digit + turn) % radix - digit) * unit))
        parts.append(lax.ppermute(value, "tm", pairs))
    for part in parts:
        value = value + part
    return value


def contract(left, right, left_dim, right_dim):
    return lax.dot_general(
        left, right, (((left_dim,), (right_dim,)), ((), ())), preferred_element_type=jnp.float32
    )


STEPS = 4 + ROUNDS
DIRECT = 2
INT_COUNT = STEPS * 4
BIAS_CENTRE = STEPS * 4


def table_kernel(chain, mask, strides, ints, bias):
    chain_pos = chain[0]
    groups = chain[1]
    partner = chain_pos ^ 1
    near_step = jnp.where(chain_pos // 2 % 2 == 0, 2, -2)
    window_groups = (
        chain_pos,
        partner,
        chain_pos + near_step,
        partner + near_step,
        chain_pos - near_step,
        partner - near_step,
    )
    same = jnp.where(chain_pos // 2 % 2 == chain_pos % 2, 1, 0)
    offs = ((1, 2, 4, 3 + 2 * same), (0, 3, 5, 4 - 2 * same))
    for g in range(2):
        query_group = window_groups[g]
        for n in range(STEPS * 4):
            ints[g, n] = 0
            bias[g, n] = jnp.float32(DEAD)
        near = []
        for w in range(WINDOWS):
            apart = jnp.abs(window_groups[w] - query_group)
            inside = (window_groups[w] >= 0) & (window_groups[w] < groups)
            near.append(jnp.where((apart <= WIN) & inside, 1, 0))
        for o in range(4):
            at = offs[g][o]
            inside = functools.reduce(
                jnp.add, [jnp.where(at == w, near[w], 0) for w in range(WINDOWS)]
            )
            for i in range(4):
                ints[g, o * 4 + i] = at * 4 + i
                bias[g, o * 4 + i] = jnp.where(inside == 1, 0.0, DEAD).astype(jnp.float32)
        counts = [jnp.int32(0)] * 4
        for w in range(WINDOWS):
            apart = window_groups[w] - query_group
            level = jnp.minimum(jnp.abs(apart), WIN)
            stride = strides[level]
            rest = lax.rem((query_group + jnp.clip(window_groups[w], 0, groups - 1)) * 4, stride)
            column = jnp.clip(apart + WIN, 0, 2 * WIN) * 4
            for i in range(4):
                row = query_group * 4 + i
                for j in range(4):
                    if w == g and i == j:
                        bias[g, BIAS_CENTRE + i * 4 + j] = jnp.float32(0.0)
                        continue
                    if i == j:
                        continue
                    total = rest + (i + j)
                    hit = functools.reduce(
                        jnp.logical_or, [total == stride * n for n in range(5)]
                    ) | (stride == 1)
                    live = (mask[row, column + j] == 1) & hit
                    if w == g:
                        bias[g, BIAS_CENTRE + i * 4 + j] = jnp.where(live, 0.0, DEAD).astype(
                            jnp.float32
                        )
                        continue
                    live = live & (near[w] == 1)

                    @pl.when(live)
                    def _(g=g, w=w, i=i, j=j, count=counts[i]):
                        ints[g, (4 + count) * 4 + i] = w * 4 + j
                        bias[g, (4 + count) * 4 + i] = jnp.float32(0.0)

                    counts[i] = counts[i] + jnp.where(live, 1, 0)
        ints[g, INT_COUNT] = functools.reduce(jnp.maximum, counts)


def live_tables(chain_pos, groups, block_mask, band_strides):
    table = pl.BlockSpec(memory_space=pltpu.SMEM)
    return pl.pallas_call(
        table_kernel,
        in_specs=[table] * 3,
        out_specs=[table] * 2,
        out_shape=[
            jax.ShapeDtypeStruct((2, INT_COUNT + 1), jnp.int32),
            jax.ShapeDtypeStruct((2, BIAS_CENTRE + 16), jnp.float32),
        ],
        name="live_tables",
    )(jnp.stack([chain_pos, jnp.int32(groups)]), block_mask, band_strides)


def fold_rows(tile, op):
    return op(tile.reshape(BLK // 8, 8, BLK), axis=0)


def attention_kernel(
    groups_here,
    ints,
    bias,
    query,
    grad,
    own_key,
    partner_key,
    near_own_key,
    near_partner_key,
    far_own_key,
    far_partner_key,
    own_value,
    partner_value,
    near_own_value,
    near_partner_value,
    far_own_value,
    far_partner_value,
    own_rows,
    pair_rows,
    near_back,
    far_back,
    local,
    gains,
    pairs,
    keys_t,
    vals_t,
    off_pairs,
    off_keys_t,
    off_vals_t,
    grads,
    centre_w,
    centre_p,
    centre_b,
    centre_d,
    off_s,
    off_d,
    extra_s,
    extra_d,
    out_t,
    top_rows,
    sum_rows,
    both,
    both_scaled,
    grad_scaled,
    gain_rows,
):
    left, right = pl.ds(0, BLK), pl.ds(BLK, BLK)
    key_windows = (
        own_key,
        partner_key,
        near_own_key,
        near_partner_key,
        far_own_key,
        far_partner_key,
    )
    value_windows = (
        own_value,
        partner_value,
        near_own_value,
        near_partner_value,
        far_own_value,
        far_partner_value,
    )
    for w in range(WINDOWS):
        for j in range(BLOCKS_HERE):
            rows = pl.ds(j * BLK, BLK)
            key = key_windows[w][rows, :]
            value = value_windows[w][rows, :]
            pairs[w * 4 + j, :, left] = key
            pairs[w * 4 + j, :, right] = value
            keys_t[w * 4 + j] = key.T
            vals_t[w * 4 + j] = value.T
    gain_rows[...] = jnp.zeros_like(gain_rows)
    grads[...] = jnp.zeros_like(grads)
    both[...] = jnp.zeros_like(both)
    both_scaled[...] = jnp.zeros_like(both_scaled)

    def put_rows(g, kind, i, tile):
        rows = pl.ds(i * BLK, BLK)
        if groups_here == 1:
            own_rows[kind, rows, :] = tile
            return

        @pl.when(g == 0)
        def _():
            own_rows[kind, rows, :] = tile

        @pl.when(g == 1)
        def _():
            pair_rows[kind, rows, :] = tile

    def rows_of(i):
        return pl.ds(i * BLK, BLK)

    def group_task(g, direct):
        centre = g * 4
        steps = 4 + direct
        all_steps = 4 + ints[g, INT_COUNT]

        def gather(s, c):
            there = pl.ds(pl.multiple_of(s * BLK, BLK), BLK)
            for i in range(4):
                at = ints[g, s * 4 + i]
                off_pairs[i, there, :] = pairs[at]
                off_keys_t[i, :, there] = keys_t[at]
                off_vals_t[i, :, there] = vals_t[at]
            return c

        lax.fori_loop(0, steps, gather, 0)
        off_span = pl.ds(0, steps * BLK)

        def loop_rest(body):
            if direct == DIRECT:
                lax.fori_loop(steps, all_steps, body, 0)

        query_all = query[g]
        grad_all = grad[g]
        for i in range(4):
            both[i, left, left] = query[g, rows_of(i), :]
            both[i, right, right] = grad[g, rows_of(i), :]
            both_scaled[i, left, left] = query[g, rows_of(i), :]
        for i in range(4):
            off_s[i, off_span, :] = contract(off_pairs[i, off_span, :], both[i], 1, 1)
        centre_keys = pairs[pl.ds(centre, 4), :, left].reshape(TOK, HEAD_DIM)
        centre_vals = pairs[pl.ds(centre, 4), :, right].reshape(TOK, HEAD_DIM)
        centre_w[...] = contract(centre_keys, query_all, 1, 1)
        centre_p[...] = contract(centre_vals, grad_all, 1, 1)
        for i in range(4):
            best = None
            for j in range(4):
                part = fold_rows(centre_w[rows_of(j), rows_of(i)], jnp.max)
                part = part + bias[g, BIAS_CENTRE + i * 4 + j]
                best = part if best is None else jnp.maximum(best, part)
            for o in range(steps):
                part = fold_rows(off_s[i, rows_of(o), left], jnp.max) + bias[g, o * 4 + i]
                best = jnp.maximum(best, part)
            top_rows[i] = best

        def rest_scores(s, c):
            for i in range(4):
                scores = contract(pairs[ints[g, s * 4 + i]], both[i], 1, 1)
                extra_s[s * 4 + i] = scores
                part = fold_rows(scores[:, :BLK], jnp.max) + bias[g, s * 4 + i]
                top_rows[i] = jnp.maximum(top_rows[i], part)
            return c

        loop_rest(rest_scores)
        tops = [jnp.max(top_rows[i], axis=0, keepdims=True) for i in range(4)]

        for i in range(4):
            total = None
            for j in range(4):
                less = tops[i] - bias[g, BIAS_CENTRE + i * 4 + j]
                weight = jnp.exp2(centre_w[rows_of(j), rows_of(i)] - less)
                centre_w[rows_of(j), rows_of(i)] = weight
                centre_b[rows_of(j), rows_of(i)] = weight.astype(jnp.bfloat16)
                part = fold_rows(weight, jnp.sum)
                total = part if total is None else total + part
            for o in range(steps):
                less = tops[i] - bias[g, o * 4 + i]
                weight = jnp.exp2(off_s[i, rows_of(o), left] - less)
                off_s[i, rows_of(o), left] = weight
                off_d[i, rows_of(o), right] = weight.astype(jnp.bfloat16)
                total = total + fold_rows(weight, jnp.sum)
            sum_rows[i] = total
        centre_vals_t = jnp.concatenate([vals_t[centre + j] for j in range(4)], axis=1)
        centre_out = contract(centre_vals_t, centre_b[...], 1, 0)
        for i in range(4):
            out_t[i] = centre_out[:, i * BLK : (i + 1) * BLK] + contract(
                off_vals_t[i, :, off_span], off_d[i, off_span, right], 1, 0
            )

        def rest_out(s, c):
            for i in range(4):
                less = tops[i] - bias[g, s * 4 + i]
                weight = jnp.exp2(extra_s[s * 4 + i, :, left] - less)
                extra_s[s * 4 + i, :, left] = weight
                weight_b = weight.astype(jnp.bfloat16)
                extra_d[s * 4 + i, :, right] = weight_b
                sum_rows[i] = sum_rows[i] + fold_rows(weight, jnp.sum)
                out_t[i] = out_t[i] + contract(vals_t[ints[g, s * 4 + i]], weight_b, 1, 0)
            return c

        loop_rest(rest_out)

        dots = []
        inverses = []
        for i in range(4):
            inverse = 1.0 / jnp.sum(sum_rows[i], axis=0, keepdims=True)
            head_out = (out_t[i] * inverse).astype(jnp.bfloat16)
            put_rows(g, 0, i, head_out.T)
            grad_t = grad[g, rows_of(i), :].T.astype(jnp.float32) * inverse
            dots.append(jnp.sum(grad_t * head_out.astype(jnp.float32), axis=0, keepdims=True))
            inverses.append(inverse)
            scaled = grad_t.astype(jnp.bfloat16).T
            grad_scaled[rows_of(i), :] = scaled
            both_scaled[i, right, right] = scaled

        for i in range(4):
            for j in range(4):
                flow = centre_p[rows_of(j), rows_of(i)] * inverses[i] - dots[i]
                centre_d[rows_of(j), rows_of(i)] = (
                    centre_w[rows_of(j), rows_of(i)] * flow
                ).astype(jnp.bfloat16)
            for o in range(steps):
                flow = off_s[i, rows_of(o), right] * inverses[i] - dots[i]
                off_d[i, rows_of(o), left] = (off_s[i, rows_of(o), left] * flow).astype(
                    jnp.bfloat16
                )
        centre_keys_t = jnp.concatenate([keys_t[centre + j] for j in range(4)], axis=1)
        centre_grad = contract(centre_keys_t, centre_d[...], 1, 0)
        for i in range(4):
            out_t[i] = centre_grad[:, i * BLK : (i + 1) * BLK] + contract(
                off_keys_t[i, :, off_span], off_d[i, off_span, left], 1, 0
            )
        place = pl.ds(centre, 4)
        grads[place, :, left] = grads[place, :, left] + contract(
            centre_d[...], query_all, 1, 0
        ).reshape(4, BLK, HEAD_DIM)
        grads[place, :, right] = grads[place, :, right] + contract(
            centre_b[...], grad_scaled[...], 1, 0
        ).reshape(4, BLK, HEAD_DIM)
        for i in range(4):
            part = contract(off_d[i, off_span, :], both_scaled[i], 1, 0)
            for o in range(steps):
                at = ints[g, o * 4 + i]
                grads[at] = grads[at] + part[o * BLK : (o + 1) * BLK]

        def rest_grads(s, c):
            for i in range(4):
                at = ints[g, s * 4 + i]
                flow = extra_s[s * 4 + i, :, right] * inverses[i] - dots[i]
                score_grad = (extra_s[s * 4 + i, :, left] * flow).astype(jnp.bfloat16)
                extra_d[s * 4 + i, :, left] = score_grad
                out_t[i] = out_t[i] + contract(keys_t[at], score_grad, 1, 0)
                grads[at] = grads[at] + contract(extra_d[s * 4 + i], both_scaled[i], 1, 0)
            return c

        loop_rest(rest_grads)
        gain_part = gain_rows[...]
        for i in range(4):
            back = (out_t[i] * SCALE).astype(jnp.bfloat16).T
            put_rows(g, 1, i, back)
            gain_part = gain_part + fold_rows(
                back.astype(jnp.float32) * query[g, rows_of(i), :].astype(jnp.float32), jnp.sum
            )
        gain_rows[...] = gain_part

    def any_task(g, carry):
        group_task(g, DIRECT)
        return carry

    lax.fori_loop(0, groups_here, any_task, 0)
    gain_sum = jnp.zeros((8, HEAD_DIM), jnp.float32)
    for n in range(WINDOWS * BLOCKS_HERE):
        gain_sum = gain_sum + fold_rows(
            grads[n, :, left] * pairs[n, :, left].astype(jnp.float32), jnp.sum
        )
    gains[0:1, :] = jnp.sum(gain_rows[...], axis=0, keepdims=True)
    gains[1:2, :] = jnp.sum(gain_sum, axis=0, keepdims=True)
    for n, (window, half, factor) in enumerate(
        ((1, left, LN2), (1, right, 1.0), (0, left, LN2), (0, right, 1.0))
    ):
        for j in range(BLOCKS_HERE):
            rows = pl.ds(j * BLK, BLK)
            local[n, rows, :] = grads[window * 4 + j, :, half] * factor
            near_back[n, rows, :] = (grads[(window + 2) * 4 + j, :, half] * factor).astype(
                jnp.bfloat16
            )
            far_back[n, rows, :] = (grads[(window + 4) * 4 + j, :, half] * factor).astype(
                jnp.bfloat16
            )


def attention_slot(slot, place, groups_here, ints, bias, query, grad, windows):
    token_block = pl.BlockSpec((groups_here, TOK, HEAD_DIM), lambda n: (0, 0, place))
    window_block = pl.BlockSpec((TOK, HEAD_DIM), lambda n: (0, slot))
    table = pl.BlockSpec(memory_space=pltpu.SMEM)
    out_token = pl.BlockSpec((2, TOK, HEAD_DIM), lambda n: (0, 0, 0))
    out_grads = pl.BlockSpec((4, TOK, HEAD_DIM), lambda n: (0, 0, 0))
    out_gains = pl.BlockSpec((2, HEAD_DIM), lambda n: (0, 0))
    tiles = WINDOWS * BLOCKS_HERE
    most = 4 + DIRECT
    return pl.pallas_call(
        functools.partial(attention_kernel, groups_here),
        grid=(1,),
        in_specs=[table, table, token_block, token_block]
        + [window_block] * (2 * WINDOWS),
        out_specs=[out_token, out_token, out_grads, out_grads, out_grads, out_gains],
        out_shape=[
            jax.ShapeDtypeStruct((2, TOK, HEAD_DIM), jnp.bfloat16),
            jax.ShapeDtypeStruct((2, TOK, HEAD_DIM), jnp.bfloat16),
            jax.ShapeDtypeStruct((4, TOK, HEAD_DIM), jnp.bfloat16),
            jax.ShapeDtypeStruct((4, TOK, HEAD_DIM), jnp.bfloat16),
            jax.ShapeDtypeStruct((4, TOK, HEAD_DIM), jnp.float32),
            jax.ShapeDtypeStruct((2, HEAD_DIM), jnp.float32),
        ],
        scratch_shapes=[
            pltpu.VMEM((tiles, BLK, 2 * BLK), jnp.bfloat16),
            pltpu.VMEM((tiles, BLK, BLK), jnp.bfloat16),
            pltpu.VMEM((tiles, BLK, BLK), jnp.bfloat16),
            pltpu.VMEM((4, most * BLK, 2 * BLK), jnp.bfloat16),
            pltpu.VMEM((4, BLK, most * BLK), jnp.bfloat16),
            pltpu.VMEM((4, BLK, most * BLK), jnp.bfloat16),
            pltpu.VMEM((tiles, BLK, 2 * BLK), jnp.float32),
            pltpu.VMEM((TOK, TOK), jnp.float32),
            pltpu.VMEM((TOK, TOK), jnp.float32),
            pltpu.VMEM((TOK, TOK), jnp.bfloat16),
            pltpu.VMEM((TOK, TOK), jnp.bfloat16),
            pltpu.VMEM((4, most * BLK, 2 * BLK), jnp.float32),
            pltpu.VMEM((4, most * BLK, 2 * BLK), jnp.bfloat16),
            pltpu.VMEM((STEPS * 4, BLK, 2 * BLK), jnp.float32),
            pltpu.VMEM((STEPS * 4, BLK, 2 * BLK), jnp.bfloat16),
            pltpu.VMEM((4, BLK, BLK), jnp.float32),
            pltpu.VMEM((4, 8, BLK), jnp.float32),
            pltpu.VMEM((4, 8, BLK), jnp.float32),
            pltpu.VMEM((4, 2 * BLK, 2 * BLK), jnp.bfloat16),
            pltpu.VMEM((4, 2 * BLK, 2 * BLK), jnp.bfloat16),
            pltpu.VMEM((TOK, HEAD_DIM), jnp.bfloat16),
            pltpu.VMEM((8, HEAD_DIM), jnp.float32),
        ],
        compiler_params=pltpu.CompilerParams(vmem_limit_bytes=40 * 1024 * 1024),
        cost_estimate=pl.CostEstimate(
            flops=groups_here * 40 * 6 * 2 * BLK**3 * 4,
            bytes_accessed=6 * 1024 * 1024,
            transcendentals=groups_here * 40 * BLK * BLK,
        ),
        name="attention_slot",
    )(ints, bias, query, grad, *windows)


def shards(query_raw, key_raw, values, query_gain, key_gain, out_grad, block_mask, band_strides):
    features = query_raw.shape[1]
    groups = lax.axis_size("tm")
    chain_pos = lax.axis_index("tm")
    even = chain_pos % 2 == 0
    all_features = features * lax.axis_size("head")
    half = 2 * HEAD_DIM

    def keep(x):
        return jnp.where(even, x[..., :half], x[..., half : 2 * half])

    def give(x):
        return jnp.where(even, x[..., half : 2 * half], x[..., :half])

    def last(x):
        return x[..., 2 * half :]

    def spread(rows, ahead=()):
        own = jnp.concatenate([keep(rows), last(rows)], axis=1)
        partner = swapped(jnp.concatenate([give(rows), last(rows)], axis=1), "tm")
        near_own, far_own = to_near(own, "tm"), to_far(own, "tm")
        partner, _ = lax.optimization_barrier((partner, ahead))
        near_partner, far_partner = to_near(partner, "tm"), to_far(partner, "tm")
        return (own, partner, near_own, near_partner, far_own, far_partner)

    value_windows = spread(values)
    query_float = query_raw.astype(jnp.float32)
    key_float = key_raw.astype(jnp.float32)
    shares = jnp.stack(
        [jnp.sum(key_float * key_float, axis=1), jnp.sum(query_float * query_float, axis=1)]
    )
    squares = lax.psum(shares, "head")
    inverses = lax.rsqrt(squares / all_features + NORM_EPSILON)
    key_inverse = inverses[0][:, None]
    query_inverse = inverses[1][:, None]
    query_unit = query_float * query_inverse
    key_unit = key_float * key_inverse
    key_normed = (key_unit * key_gain[None, :]).astype(jnp.bfloat16)
    key_windows = spread(key_normed, value_windows[2:5:2])
    windows = lax.optimization_barrier(key_windows + value_windows)

    query_scaled = (query_unit * (query_gain * (SCALE * LOG2E))[None, :]).astype(jnp.bfloat16)
    given_query, _ = lax.optimization_barrier(
        (jnp.stack([give(query_scaled), give(out_grad)]), key_windows[1])
    )
    given = swapped(given_query, "tm")
    query_pair = jnp.stack([keep(query_scaled), given[0]])
    grad_pair = jnp.stack([keep(out_grad), given[1]])
    query_last = last(query_scaled)[None]
    grad_last = last(out_grad)[None]
    ints, bias = live_tables(chain_pos, groups, block_mask, band_strides)

    def received(result):
        return (to_near(result[2], "tm"), to_far(result[3], "tm"))

    result_last = attention_slot(2, 0, 1, ints, bias, query_last, grad_last, windows)
    received_last = received(result_last)
    result_first = attention_slot(0, 0, 2, ints, bias, query_pair, grad_pair, windows)
    received_first = received(result_first)
    query_gated, rows_to_give, received_last = lax.optimization_barrier(
        (query_pair, result_first[1], received_last)
    )
    rows_first = swapped(rows_to_give, "tm")
    result_second = attention_slot(1, 1, 2, ints, bias, query_gated, grad_pair, windows)
    received_second = received(result_second)
    gains = (result_first[5], result_second[5], result_last[5])

    def placed(mine, theirs, rest):
        first = jnp.where(even, mine, theirs)
        second = jnp.where(even, theirs, mine)
        return jnp.concatenate([first, second, rest], axis=-1)

    taken = jnp.concatenate([gains[0], gains[1]], axis=1)
    gains = placed(taken, jnp.zeros_like(taken), gains[2])
    gains = gains * jnp.stack([1.0 / (query_gain * (SCALE * LOG2E)), LN2 / key_gain])
    gains = summed_over_digit(gains, 1, 2)

    def part_sum(result, pair, start):
        stop = start + 2
        return (
            result[4][start:stop]
            + pair[0][start:stop].astype(jnp.float32)
            + pair[1][start:stop].astype(jnp.float32)
        )

    results = (result_first, result_second, result_last)
    give_first, give_last = (
        part_sum(result, pair, 0).astype(jnp.bfloat16)
        for result, pair in ((result_first, received_first), (result_last, received_last))
    )
    gains, rows_to_give, give_first, give_last = lax.optimization_barrier(
        (gains, result_second[1], give_first, give_last)
    )
    rows_second = swapped(rows_to_give, "tm")
    gains, rows_second = lax.optimization_barrier((gains, rows_second))
    gains = summed_over_digit(gains, 2, 4)
    give_second = part_sum(result_second, received_second, 0).astype(jnp.bfloat16)
    pairs = (received_first, received_second, received_last)
    kept_grads = [part_sum(result, pair, 2) for result, pair in zip(results, pairs)]
    given_grads = [
        swapped(part, "tm").astype(jnp.float32) for part in (give_first, give_second, give_last)
    ]
    gains, given_grads = lax.optimization_barrier((gains, given_grads))
    gains = summed_over_digit(gains, 8, 4)

    rows = placed(
        jnp.concatenate([result_first[0], result_second[0]], axis=2),
        jnp.concatenate([rows_first, rows_second], axis=2),
        result_last[0],
    )
    attended = rows[0]
    grad_query = rows[1].astype(jnp.float32)
    grads = placed(
        jnp.concatenate([kept_grads[0], kept_grads[1]], axis=2),
        jnp.concatenate([given_grads[0], given_grads[1]], axis=2),
        kept_grads[2] + given_grads[2],
    )
    grad_key = grads[0]
    grad_value = grads[1].astype(jnp.bfloat16)
    query_back = grad_query * query_gain[None, :]
    key_back = grad_key * key_gain[None, :]
    inner = lax.psum(
        jnp.stack([jnp.sum(query_back * query_unit, axis=1), jnp.sum(key_back * key_unit, axis=1)]),
        "head",
    )
    inner = inner / all_features
    query_grad = (query_inverse * (query_back - query_unit * inner[0][:, None])).astype(jnp.bfloat16)
    key_grad = (key_inverse * (key_back - key_unit * inner[1][:, None])).astype(jnp.bfloat16)
    return (attended, query_grad, key_grad, grad_value, gains[0], gains[1])


def solution(mesh):
    placed = (
        P("tm", "head"),
        P("tm", "head"),
        P("tm", "head"),
        P("head"),
        P("head"),
        P("tm", "head"),
        P(),
        P(),
    )
    return jax.shard_map(
        shards,
        mesh=mesh,
        in_specs=placed,
        out_specs=(
            P("tm", "head"),
            P("tm", "head"),
            P("tm", "head"),
            P("tm", "head"),
            P("head"),
            P("head"),
        ),
        check_vma=False,
    )
```

time: 151 us -> 146 us (0.967); the launches traced: 149 us -> 146 us
  waiting for transfers between devices: 30.7 us -> 8.54 us
  starting transfers between devices: 56.5 us -> 67.9 us
  Pallas kernels: 24.8 us -> 32.8 us
  other arithmetic: 16.3 us -> 12.6 us
  local copies, waits for them, and re-layouts: 6.9 us -> 10.2 us
    ppermute x7 -> x8, waiting for transfers between devices: 17.5 us -> 6.88 us  [swapped(): lax.ppermute(value, axis, [(s, s ^ 1) for s in range(lax.axis_size(axis))])]
    ppermute x5 -> x7, waiting for transfers between devices: 8.96 us -> 0.02 us  [to_near(): lax.ppermute(value, axis, [(s, s ^ 2) for s in range(lax.axis_size(axis))])]
    ppermute x5 -> x7, starting transfers between devices: 21.5 us -> 27.9 us  [to_near(): lax.ppermute(value, axis, [(s, s ^ 2) for s in range(lax.axis_size(axis))])]
    pallas_call x3, Pallas kernels: 24.8 us -> 29.1 us  [attention_slot(): pl.pallas_call(functools.partial(attention_kernel, groups_here), grid=(1,...]
    pallas_call x0 -> x1, Pallas kernels: none -> 3.68 us  [live_tables(): pl.pallas_call(table_kernel, in_specs=[table] * 3, out_specs=[table] * 2,...]
    ppermute x5 -> x7, starting transfers between devices: 3.64 us -> 6.37 us  [to_far(): lax.ppermute(value, axis, [(s, d) for s, d in pairs if 0 <= d < count])]
    ppermute x7, waiting for transfers between devices: 4.23 us -> 1.63 us  [summed_over_digit(): parts.append(lax.ppermute(value, 'tm', pairs))]
    another operation x2, local copies, waits for them, and re-layouts: 0.01 us -> 2.55 us  [shards(): jnp.stack([1.0 / (query_gain * (SCALE * LOG2E)), LN2 / key_gain])]
  transfers between devices with their start and end apart: 24 -> 29, of which waited for: 8 -> 4; matrix products, arithmetic and copies ran while one was open for 9% -> 11% of each run, Pallas kernels for 13% -> 22%
where the time goes in v1:
time: 146 us
  starting transfers between devices  67.9 us (47%)
  Pallas kernels  32.8 us (22%)
  blocking collectives  12.8 us (9%)
  other arithmetic  12.6 us (9%)
  local copies, waits for them, and re-layouts  10.2 us (7%)
  waiting for transfers between devices  8.54 us (6%)
    pallas_call x3, Pallas kernels, attention_slot(): pl.pallas_call(functools.partial(attention_kernel, groups_here), grid=(1,...  29.1 us
    ppermute x7, starting transfers between devices, to_near(): lax.ppermute(value, axis, [(s, s ^ 2) for s in range(lax.axis_size(axis))])  27.9 us
    ppermute x7, starting transfers between devices, summed_over_digit(): parts.append(lax.ppermute(value, 'tm', pairs))  17.4 us
    ppermute x8, starting transfers between devices, swapped(): lax.ppermute(value, axis, [(s, s ^ 1) for s in range(lax.axis_size(axis))])  16.1 us
    psum x1, blocking collectives, shards(): squares = lax.psum(shares, 'head')  7.07 us
    ppermute x8, waiting for transfers between devices, swapped(): lax.ppermute(value, axis, [(s, s ^ 1) for s in range(lax.axis_size(axis))])  6.88 us
    ppermute x7, starting transfers between devices, to_far(): lax.ppermute(value, axis, [(s, d) for s, d in pairs if 0 <= d < count])  6.37 us
    psum x1, blocking collectives, shards(): lax.psum(jnp.stack([jnp.sum(query_back * query_unit, axis=1), jnp.sum(key...  5.77 us
  transfers between devices with their start and end apart: 29, of which 4 were waited for; matrix products, arithmetic and copies ran while one was open for 11% of the time, Pallas kernels for 22%

profile of v1, /device:TPU:0, one launch (start us, length us, event | category | flops | bytes accessed | tf_op | source)
XLA Modules:
  0.0 146.0 jit_solution(17804305166045830860)
XLA Ops:
  0.7 1.4 fusion.17
  2.1 1.3 fusion.11
  3.4 7.1 %psum.14 = f32[2,512]{1,0:T(2,128)S(1)} all-reduce(f32[2,512]{1,0:T(2,128)S(1)} %pad_maximum_fusion.10), channel_id=1, replica_groups=mesh['tm'=32,'head'=4] {'head'}, use_global_device_ids=true, to_apply=%region_2.3 | all-reduce | flops 1024 | bytes 8192 | tf_op jit(solution)/shard_map/psum | solution.py:514
  10.8 0.8 slice-done
  11.7 2.0 %collective-permute-start.1 = (bf16[512,384]{1,0:T(8,128)(2,1)S(1)}, bf16[512,384]{1,0:T(8,128)(2,1)S(1)}, u32[]{:S(2)}, u32[]{:S(2)}) collective-permute-start(bf16[512,384]{1,0:T(8,128)(2,1)S(1)} %get-tuple-element.63.own_value), channel_id=1, source_target_pairs={{0,8},{4,12},{8,0},{12,4},{16,24},{20,28},{24,16},{28,20},{32,40},... | collective-permute-start | bytes 1179656 | tf_op jit(solution)/shard_map/ppermute | solution.py:26
  14.5 3.0 %collective-permute-start = (bf16[512,384]{1,0:T(8,128)(2,1)S(1)}, bf16[512,384]{1,0:T(8,128)(2,1)S(1)}, u32[]{:S(2)}, u32[]{:S(2)}) collective-permute-start(bf16[512,384]{1,0:T(8,128)(2,1)S(1)} %get-tuple-element.122), channel_id=1, source_target_pairs={{0,4},{4,0},{8,12},{12,8},{16,20},{20,16},{24,28},{28,24},{32,36},... | collective-permute-start | bytes 1179656 | tf_op jit(solution)/shard_map/ppermute | solution.py:36
  18.1 4.8 %collective-permute-start.4 = (bf16[512,384]{1,0:T(8,128)(2,1)S(1)}, bf16[512,384]{1,0:T(8,128)(2,1)S(1)}, u32[]{:S(2)}, u32[]{:S(2)}) collective-permute-start(bf16[512,384]{1,0:T(8,128)(2,1)S(1)} %get-tuple-element.57.own_key), channel_id=1, source_target_pairs={{0,8},{4,12},{8,0},{12,4},{16,24},{20,28},{24,16},{28,20},{32,40},... | collective-permute-start | bytes 1179656 | tf_op jit(solution)/shard_map/ppermute | solution.py:26
  23.7 0.9 select_bitcast_fusion.3
  24.6 0.8 select_bitcast_fusion
  26.8 1.4 collective-permute-done.partner_key
  28.1 4.8 %collective-permute-start.5 = (bf16[512,384]{1,0:T(8,128)(2,1)S(1)}, bf16[512,384]{1,0:T(8,128)(2,1)S(1)}, u32[]{:S(2)}, u32[]{:S(2)}) collective-permute-start(bf16[512,384]{1,0:T(8,128)(2,1)S(1)} %collective-permute-done.partner_key), channel_id=1, source_target_pairs={{0,8},{4,12},{8,0},{12,4},{16,24},{20,28},{24,16},{28,20},{32,40},... | collective-permute-start | bytes 1179656 | tf_op jit(solution)/shard_map/ppermute | solution.py:26
  32.9 1.4 collective-permute-start.7
  34.3 1.4 collective-permute-start.10
  35.7 4.9 %collective-permute-start.9 = (bf16[512,384]{1,0:T(8,128)(2,1)S(1)}, bf16[512,384]{1,0:T(8,128)(2,1)}, u32[]{:S(2)}, u32[]{:S(2)}) collective-permute-start(bf16[512,384]{1,0:T(8,128)(2,1)S(1)} %collective-permute-done.8.partner_value), channel_id=1, source_target_pairs={{0,8},{4,12},{8,0},{12,4},{16,24},{20,28},{24,16},{28,20},{32,40},... | collective-permute-start | bytes 1179656 | tf_op jit(solution)/shard_map/ppermute | solution.py:26
  41.2 1.4 copy.14.mask
  42.7 1.3 stack.66
  43.9 1.3 stack.67
  45.2 3.7 %live_tables.1 = (s32[2,65]{1,0:T(2,128)}, f32[2,80]{1,0:T(2,128)}) custom-call(s32[2]{0:T(128)} %pad_add_fusion.chain, s32[128,20]{1,0:T(8,128)} %copy.14.mask, s32[3]{0:T(128)} %strides.1), custom_call_target="tpu_custom_call" | custom-call | tf_op jit(solution)/shard_map/live_tables/pallas_call | solution.py:135
  48.9 1.1 pad_maximum_fusion.3
  50.0 3.3 %collective-permute-start.3 = (bf16[2,512,256]{2,1,0:T(8,128)(2,1)S(1)}, bf16[2,512,256]{2,1,0:T(8,128)(2,1)S(1)}, u32[]{:S(2)}, u32[]{:S(2)}) collective-permute-start(bf16[2,512,256]{2,1,0:T(8,128)(2,1)S(1)} %pad_maximum_fusion.3), channel_id=1, source_target_pairs={{0,4},{4,0},{8,12},{12,8},{16,20},{20,16},{24,28},{28,24},{32,36},... | collective-permute-start | bytes 1572872 | tf_op jit(solution)/shard_map/ppermute | solution.py:36
  53.3 1.0 slice_bitcast_fusion.3
  54.4 6.5 %attention_slot.4 = (bf16[2,512,128]{2,1,0:T(8,128)(2,1)S(1)}, bf16[2,512,128]{2,1,0:T(8,128)(2,1)}, bf16[4,512,128]{2,1,0:T(8,128)(2,1)S(1)}, bf16[4,512,128]{2...) custom-call(s32[2,65]{1,0:T(2,128)S(1)} %copy-done, f32[2,80]{1,0:T(2,128)S(1)} %copy-done.1, ...), custom_call_target="tpu_custom_call" | custom-call | flops 4026531840 | bytes 6291456 | tf_op jit(solution)/shard_map/attention_slot/pallas_call | solution.py:435
  60.9 0.8 collective-permute-start.11
  61.7 0.9 collective-permute-start.12
  62.7 11.2 %attention_slot.3 = (bf16[2,512,128]{2,1,0:T(8,128)(2,1)S(1)}, bf16[2,512,128]{2,1,0:T(8,128)(2,1)S(1)}, bf16[4,512,128]{2,1,0:T(8,128)(2,1)S(1)}, bf16[4,512,12...) custom-call(s32[2,65]{1,0:T(2,128)S(1)} %copy-done, f32[2,80]{1,0:T(2,128)S(1)} %copy-done.1, ...), custom_call_target="tpu_custom_call" | custom-call | flops 8053063680 | bytes 6291456 | tf_op jit(solution)/shard_map/attention_slot/pallas_call | solution.py:435
  74.0 6.4 %collective-permute-start.15 = (bf16[4,512,128]{2,1,0:T(8,128)(2,1)S(1)}, bf16[4,512,128]{2,1,0:T(8,128)(2,1)S(1)}, u32[]{:S(2)}, u32[]{:S(2)}) collective-permute-start(bf16[4,512,128]{2,1,0:T(8,128)(2,1)S(1)} %get-tuple-element.81), channel_id=1, source_target_pairs={{0,8},{4,12},{8,0},{12,4},{16,24},{20,28},{24,16},{28,20},{32,40},... | collective-permute-start | bytes 1572872 | tf_op jit(solution)/shard_map/ppermute | solution.py:26
  80.4 0.7 collective-permute-start.16
  81.2 11.4 %attention_slot.5 = (bf16[2,512,128]{2,1,0:T(8,128)(2,1)S(1)}, bf16[2,512,128]{2,1,0:T(8,128)(2,1)S(1)}, bf16[4,512,128]{2,1,0:T(8,128)(2,1)S(1)}, bf16[4,512,12...) custom-call(s32[2,65]{1,0:T(2,128)S(1)} %copy-done, f32[2,80]{1,0:T(2,128)S(1)} %copy-done.1, ...), custom_call_target="tpu_custom_call" | custom-call | flops 8053063680 | bytes 6291456 | tf_op jit(solution)/shard_map/attention_slot/pallas_call | solution.py:435
  92.6 1.9 %collective-permute-start.14 = (f32[2,640]{1,0:T(2,128)S(1)}, f32[2,640]{1,0:T(2,128)S(1)}, u32[]{:S(2)}, u32[]{:S(2)}) collective-permute-start(f32[2,640]{1,0:T(2,128)S(1)} %maximum_multiply_fusion), channel_id=1, source_target_pairs={{0,4},{4,0},{8,12},{12,8},{16,20},{20,16},{24,28},{28,24},{32,36},... | collective-permute-start | bytes 15368 | tf_op jit(solution)/shard_map/ppermute | solution.py:46
  94.5 1.7 %collective-permute-start.13 = (bf16[2,512,128]{2,1,0:T(8,128)(2,1)S(1)}, bf16[2,512,128]{2,1,0:T(8,128)(2,1)S(1)}, u32[]{:S(2)}, u32[]{:S(2)}) collective-permute-start(bf16[2,512,128]{2,1,0:T(8,128)(2,1)S(1)} %get-tuple-element.75), channel_id=1, source_target_pairs={{0,4},{4,0},{8,12},{12,8},{16,20},{20,16},{24,28},{28,24},{32,36},... | collective-permute-start | bytes 786440 | tf_op jit(solution)/shard_map/ppermute | solution.py:36
  96.3 1.6 %collective-permute-done.14 = f32[2,640]{1,0:T(2,128)S(1)} collective-permute-done((f32[2,640]{1,0:T(2,128)S(1)}, f32[2,640]{1,0:T(2,128)S(1)}, u32[]{:S(2)}, u32[]{:S(2)}) %collective-permute-start.14) | collective-permute-done | bytes 5152 | tf_op jit(solution)/shard_map/ppermute | solution.py:46
  98.1 1.9 %collective-permute-start.17 = (bf16[2,512,128]{2,1,0:T(8,128)(2,1)S(1)}, bf16[2,512,128]{2,1,0:T(8,128)(2,1)S(1)}, u32[]{:S(2)}, u32[]{:S(2)}) collective-permute-start(bf16[2,512,128]{2,1,0:T(8,128)(2,1)S(1)} %get-tuple-element.87), channel_id=1, source_target_pairs={{0,4},{4,0},{8,12},{12,8},{16,20},{20,16},{24,28},{28,24},{32,36},... | collective-permute-start | bytes 786440 | tf_op jit(solution)/shard_map/ppermute | solution.py:36
  100.1 4.3 %collective-permute-start.18 = (bf16[4,512,128]{2,1,0:T(8,128)(2,1)S(1)}, bf16[4,512,128]{2,1,0:T(8,128)(2,1)S(1)}, u32[]{:S(2)}, u32[]{:S(2)}) collective-permute-start(bf16[4,512,128]{2,1,0:T(8,128)(2,1)S(1)} %get-tuple-element.91), channel_id=1, source_target_pairs={{0,8},{4,12},{8,0},{12,4},{16,24},{20,28},{24,16},{28,20},{32,40},... | collective-permute-start | bytes 1572872 | tf_op jit(solution)/shard_map/ppermute | solution.py:26
  104.4 0.7 collective-permute-start.19
  105.2 3.1 %collective-permute-start.25 = (bf16[2,512,128]{2,1,0:T(8,128)(2,1)S(1)}, bf16[2,512,128]{2,1,0:T(8,128)(2,1)S(1)}, u32[]{:S(2)}, u32[]{:S(2)}) collective-permute-start(bf16[2,512,128]{2,1,0:T(8,128)(2,1)S(1)} %add_convert_fusion.1), channel_id=1, source_target_pairs={{0,4},{4,0},{8,12},{12,8},{16,20},{20,16},{24,28},{28,24},{32,36},... | collective-permute-start | bytes 786440 | tf_op jit(solution)/shard_map/ppermute | solution.py:36
  108.9 5.4 %collective-permute-start.20 = (f32[2,640]{1,0:T(2,128)S(1)}, f32[2,640]{1,0:T(2,128)S(1)}, u32[]{:S(2)}, u32[]{:S(2)}) collective-permute-start(f32[2,640]{1,0:T(2,128)S(1)} %add.77), channel_id=1, source_target_pairs={{0,8},{4,12},{8,16},{12,20},{16,24},{20,28},{24,0},{28,4},{32,40},... | collective-permute-start | bytes 15368 | tf_op jit(solution)/shard_map/ppermute | solution.py:46
  114.6 0.9 slice_bitcast_fusion.2
  115.6 3.7 %collective-permute-start.21 = (f32[2,640]{1,0:T(2,128)S(1)}, f32[2,640]{1,0:T(2,128)S(1)}, u32[]{:S(2)}, u32[]{:S(2)}) collective-permute-start(f32[2,640]{1,0:T(2,128)S(1)} %add.77), channel_id=1, source_target_pairs={{0,16},{4,20},{8,24},{12,28},{16,0},{20,4},{24,8},{28,12},{32,48},... | collective-permute-start | bytes 15368 | tf_op jit(solution)/shard_map/ppermute | solution.py:46
  119.3 1.1 collective-permute-start.22
  120.6 2.0 %collective-permute-start.24 = (bf16[2,512,128]{2,1,0:T(8,128)(2,1)S(1)}, bf16[2,512,128]{2,1,0:T(8,128)(2,1)S(1)}, u32[]{:S(2)}, u32[]{:S(2)}) collective-permute-start(bf16[2,512,128]{2,1,0:T(8,128)(2,1)S(1)} %get-tuple-element.107), channel_id=1, source_target_pairs={{0,4},{4,0},{8,12},{12,8},{16,20},{20,16},{24,28},{28,24},{32,36},... | collective-permute-start | bytes 786440 | tf_op jit(solution)/shard_map/ppermute | solution.py:36
  123.1 5.4 %collective-permute-done.24 = bf16[2,512,128]{2,1,0:T(8,128)(2,1)S(1)} collective-permute-done((bf16[2,512,128]{2,1,0:T(8,128)(2,1)S(1)}, bf16[2,512,128]{2,1,0:T(8,128)(2,1)S(1)}, u32[]{:S(2)}, u32[]{:S(2)}) %collective-permute-start.24) | collective-permute-done | bytes 262176 | tf_op jit(solution)/shard_map/ppermute | solution.py:36
  128.6 1.9 %collective-permute-start.26 = (f32[2,640]{1,0:T(2,128)S(1)}, f32[2,640]{1,0:T(2,128)S(1)}, u32[]{:S(2)}, u32[]{:S(2)}) collective-permute-start(f32[2,640]{1,0:T(2,128)S(1)} %add_add_fusion.2), channel_id=1, source_target_pairs={{0,32},{4,36},{8,40},{12,44},{16,48},{20,52},{24,56},{28,60},{32,6... | collective-permute-start | bytes 15368 | tf_op jit(solution)/shard_map/ppermute | solution.py:46
  130.5 3.0 %collective-permute-start.27 = (f32[2,640]{1,0:T(2,128)S(1)}, f32[2,640]{1,0:T(2,128)S(1)}, u32[]{:S(2)}, u32[]{:S(2)}) collective-permute-start(f32[2,640]{1,0:T(2,128)S(1)} %add_add_fusion.2), channel_id=1, source_target_pairs={{0,64},{4,68},{8,72},{12,76},{16,80},{20,84},{24,88},{28,92},{32,9... | collective-permute-start | bytes 15368 | tf_op jit(solution)/shard_map/ppermute | solution.py:46
  134.4 0.9 copy-done.3
  135.7 5.8 %psum.15 = f32[2,512]{1,0:T(2,128)S(1)} all-reduce(f32[2,512]{1,0:T(2,128)S(1)} %pad_maximum_fusion.11), channel_id=1, replica_groups=mesh['tm'=32,'head'=4] {'head'}, use_global_device_ids=true, to_apply=%region_5.6 | all-reduce | flops 1024 | bytes 8192 | tf_op jit(solution)/shard_map/psum | solution.py:604
  141.5 1.2 fusion.16
  143.3 1.2 fusion.10
  144.5 0.9 fusion.21
  (112 shorter events, 9.4 us)
Async XLA Ops:
  0.6 9.8 %copy-start.2 = (bf16[512,640]{1,0:T(8,128)(2,1)S(1)}, bf16[512,640]{1,0:T(8,128)(2,1)}, u32[]{:S(2)}) copy-start(bf16[512,640]{1,0:T(8,128)(2,1)} %param.9) | copy-start | bytes 1966084
  0.6 9.8 %copy-start.14 = (f32[640]{0:T(1024)S(1)}, f32[640]{0:T(1024)}, u32[]{:S(2)}) copy-start(f32[640]{0:T(1024)} %param.12) | copy-start | bytes 7684
  0.7 10.0 %copy-start.12 = (bf16[512,640]{1,0:T(8,128)(2,1)S(1)}, bf16[512,640]{1,0:T(8,128)(2,1)}, u32[]{:S(2)}) copy-start(bf16[512,640]{1,0:T(8,128)(2,1)} %param.10) | copy-start | bytes 1966084
  10.7 0.9 slice-start
  11.6 11.2 %copy-start.15 = (f32[640]{0:T(1024)S(1)}, f32[640]{0:T(1024)}, u32[]{:S(2)}) copy-start(f32[640]{0:T(1024)} %param.11) | copy-start | bytes 7684
  11.6 11.8 %copy-start.4 = (bf16[512,640]{1,0:T(8,128)(2,1)S(1)}, bf16[512,640]{1,0:T(8,128)(2,1)}, u32[]{:S(2)}) copy-start(bf16[512,640]{1,0:T(8,128)(2,1)} %param.8) | copy-start | bytes 1966084
  11.7 13.8 %collective-permute-start.1 = (bf16[512,384]{1,0:T(8,128)(2,1)S(1)}, bf16[512,384]{1,0:T(8,128)(2,1)S(1)}, u32[]{:S(2)}, u32[]{:S(2)}) collective-permute-start(bf16[512,384]{1,0:T(8,128)(2,1)S(1)} %get-tuple-element.63.own_value), channel_id=1, source_target_pairs={{0,8},{4,12},{8,0},{12,4},{16,24},{20,28},{24,16},{28,20},{32,40},... | collective-permute-start | bytes 1179656 | tf_op jit(solution)/shard_map/ppermute | solution.py:26
  13.7 13.1 %collective-permute-start.2 = (bf16[512,384]{1,0:T(8,128)(2,1)S(1)}, bf16[512,384]{1,0:T(8,128)(2,1)S(1)}, u32[]{:S(2)}, u32[]{:S(2)}) collective-permute-start(bf16[512,384]{1,0:T(8,128)(2,1)S(1)} %get-tuple-element.63.own_value), channel_id=1, source_target_pairs={{8,16},{12,20},{16,8},{20,12},{24,32},{28,36},{32,24},{36,28},{40,... | collective-permute-start | bytes 1179656 | tf_op jit(solution)/shard_map/ppermute | solution.py:32
  14.5 10.1 %copy-start.13 = (bf16[512,640]{1,0:T(8,128)(2,1)S(1)}, bf16[512,640]{1,0:T(8,128)(2,1)}, u32[]{:S(2)}) copy-start(bf16[512,640]{1,0:T(8,128)(2,1)} %param.13) | copy-start | bytes 1966084
  14.5 13.6 %collective-permute-start = (bf16[512,384]{1,0:T(8,128)(2,1)S(1)}, bf16[512,384]{1,0:T(8,128)(2,1)S(1)}, u32[]{:S(2)}, u32[]{:S(2)}) collective-permute-start(bf16[512,384]{1,0:T(8,128)(2,1)S(1)} %get-tuple-element.122), channel_id=1, source_target_pairs={{0,4},{4,0},{8,12},{12,8},{16,20},{20,16},{24,28},{28,24},{32,36},... | collective-permute-start | bytes 1179656 | tf_op jit(solution)/shard_map/ppermute | solution.py:36
  17.5 16.8 %collective-permute-start.8 = (bf16[512,384]{1,0:T(8,128)(2,1)S(1)}, bf16[512,384]{1,0:T(8,128)(2,1)S(1)}, u32[]{:S(2)}, u32[]{:S(2)}) collective-permute-start(bf16[512,384]{1,0:T(8,128)(2,1)S(1)} %get-tuple-element.120), channel_id=1, source_target_pairs={{0,4},{4,0},{8,12},{12,8},{16,20},{20,16},{24,28},{28,24},{32,36},... | collective-permute-start | bytes 1179656 | tf_op jit(solution)/shard_map/ppermute | solution.py:36
  18.1 17.6 %collective-permute-start.4 = (bf16[512,384]{1,0:T(8,128)(2,1)S(1)}, bf16[512,384]{1,0:T(8,128)(2,1)S(1)}, u32[]{:S(2)}, u32[]{:S(2)}) collective-permute-start(bf16[512,384]{1,0:T(8,128)(2,1)S(1)} %get-tuple-element.57.own_key), channel_id=1, source_target_pairs={{0,8},{4,12},{8,0},{12,4},{16,24},{20,28},{24,16},{28,20},{32,40},... | collective-permute-start | bytes 1179656 | tf_op jit(solution)/shard_map/ppermute | solution.py:26
  23.7 12.0 %copy-start.9 = (bf16[512,640]{1,0:T(8,128)(2,1)}, bf16[512,640]{1,0:T(8,128)(2,1)S(1)}, u32[]{:S(2)}) copy-start(bf16[512,640]{1,0:T(8,128)(2,1)S(1)} %fusion.6) | copy-start | bytes 1966084
  25.5 24.5 %collective-permute-start.6 = (bf16[512,384]{1,0:T(8,128)(2,1)S(1)}, bf16[512,384]{1,0:T(8,128)(2,1)S(1)}, u32[]{:S(2)}, u32[]{:S(2)}) collective-permute-start(bf16[512,384]{1,0:T(8,128)(2,1)S(1)} %get-tuple-element.57.own_key), channel_id=1, source_target_pairs={{8,16},{12,20},{16,8},{20,12},{24,32},{28,36},{32,24},{36,28},{40,... | collective-permute-start | bytes 1179656 | tf_op jit(solution)/shard_map/ppermute | solution.py:32
  28.1 26.2 %collective-permute-start.5 = (bf16[512,384]{1,0:T(8,128)(2,1)S(1)}, bf16[512,384]{1,0:T(8,128)(2,1)S(1)}, u32[]{:S(2)}, u32[]{:S(2)}) collective-permute-start(bf16[512,384]{1,0:T(8,128)(2,1)S(1)} %collective-permute-done.partner_key), channel_id=1, source_target_pairs={{0,8},{4,12},{8,0},{12,4},{16,24},{20,28},{24,16},{28,20},{32,40},... | collective-permute-start | bytes 1179656 | tf_op jit(solution)/shard_map/ppermute | solution.py:26
  32.9 21.4 %collective-permute-start.7 = (bf16[512,384]{1,0:T(8,128)(2,1)S(1)}, bf16[512,384]{1,0:T(8,128)(2,1)}, u32[]{:S(2)}, u32[]{:S(2)}) collective-permute-start(bf16[512,384]{1,0:T(8,128)(2,1)S(1)} %collective-permute-done.partner_key), channel_id=1, source_target_pairs={{8,16},{12,20},{16,8},{20,12},{24,32},{28,36},{32,24},{36,28},{40,... | collective-permute-start | bytes 1179656 | tf_op jit(solution)/shard_map/ppermute | solution.py:32
  34.3 20.0 %collective-permute-start.10 = (bf16[512,384]{1,0:T(8,128)(2,1)S(1)}, bf16[512,384]{1,0:T(8,128)(2,1)}, u32[]{:S(2)}, u32[]{:S(2)}) collective-permute-start(bf16[512,384]{1,0:T(8,128)(2,1)S(1)} %collective-permute-done.8.partner_value), channel_id=1, source_target_pairs={{8,16},{12,20},{16,8},{20,12},{24,32},{28,36},{32,24},{36,28},{40,... | collective-permute-start | bytes 1179656 | tf_op jit(solution)/shard_map/ppermute | solution.py:32
  35.7 18.6 %collective-permute-start.9 = (bf16[512,384]{1,0:T(8,128)(2,1)S(1)}, bf16[512,384]{1,0:T(8,128)(2,1)}, u32[]{:S(2)}, u32[]{:S(2)}) collective-permute-start(bf16[512,384]{1,0:T(8,128)(2,1)S(1)} %collective-permute-done.8.partner_value), channel_id=1, source_target_pairs={{0,8},{4,12},{8,0},{12,4},{16,24},{20,28},{24,16},{28,20},{32,40},... | collective-permute-start | bytes 1179656 | tf_op jit(solution)/shard_map/ppermute | solution.py:26
  48.9 5.5 %copy-start = (s32[2,65]{1,0:T(2,128)S(1)}, s32[2,65]{1,0:T(2,128)}, u32[]{:S(2)}) copy-start(s32[2,65]{1,0:T(2,128)} %get-tuple-element.53.ints) | copy-start | bytes 1564
  48.9 5.4 %copy-start.1 = (f32[2,80]{1,0:T(2,128)S(1)}, f32[2,80]{1,0:T(2,128)}, u32[]{:S(2)}) copy-start(f32[2,80]{1,0:T(2,128)} %get-tuple-element.54.bias) | copy-start | bytes 1924
  50.0 12.5 %collective-permute-start.3 = (bf16[2,512,256]{2,1,0:T(8,128)(2,1)S(1)}, bf16[2,512,256]{2,1,0:T(8,128)(2,1)S(1)}, u32[]{:S(2)}, u32[]{:S(2)}) collective-permute-start(bf16[2,512,256]{2,1,0:T(8,128)(2,1)S(1)} %pad_maximum_fusion.3), channel_id=1, source_target_pairs={{0,4},{4,0},{8,12},{12,8},{16,20},{20,16},{24,28},{28,24},{32,36},... | collective-permute-start | bytes 1572872 | tf_op jit(solution)/shard_map/ppermute | solution.py:36
  54.4 8.2 %copy-start.11 = (bf16[1,512,256]{2,1,0:T(8,128)(2,1)S(1)}, bf16[1,512,256]{2,1,0:T(8,128)(2,1)}, u32[]{:S(2)}) copy-start(bf16[1,512,256]{2,1,0:T(8,128)(2,1)} %get-tuple-element.112) | copy-start | bytes 786436
  60.9 1.8 %copy-start.10 = (bf16[1,512,256]{2,1,0:T(8,128)(2,1)S(1)}, bf16[1,512,256]{2,1,0:T(8,128)(2,1)}, u32[]{:S(2)}) copy-start(bf16[1,512,256]{2,1,0:T(8,128)(2,1)} %get-tuple-element.110) | copy-start | bytes 786436
  60.9 20.3 %collective-permute-start.11 = (bf16[4,512,128]{2,1,0:T(8,128)(2,1)S(1)}, bf16[4,512,128]{2,1,0:T(8,128)(2,1)S(1)}, u32[]{:S(2)}, u32[]{:S(2)}) collective-permute-start(bf16[4,512,128]{2,1,0:T(8,128)(2,1)S(1)} %get-tuple-element.71), channel_id=1, source_target_pairs={{0,8},{4,12},{8,0},{12,4},{16,24},{20,28},{24,16},{28,20},{32,40},... | collective-permute-start | bytes 1572872 | tf_op jit(solution)/shard_map/ppermute | solution.py:26
  61.7 19.5 %collective-permute-start.12 = (bf16[4,512,128]{2,1,0:T(8,128)(2,1)S(1)}, bf16[4,512,128]{2,1,0:T(8,128)(2,1)S(1)}, u32[]{:S(2)}, u32[]{:S(2)}) collective-permute-start(bf16[4,512,128]{2,1,0:T(8,128)(2,1)S(1)} %get-tuple-element.72), channel_id=1, source_target_pairs={{8,16},{12,20},{16,8},{20,12},{24,32},{28,36},{32,24},{36,28},{40,... | collective-permute-start | bytes 1572872 | tf_op jit(solution)/shard_map/ppermute | solution.py:32
  74.0 24.0 %collective-permute-start.15 = (bf16[4,512,128]{2,1,0:T(8,128)(2,1)S(1)}, bf16[4,512,128]{2,1,0:T(8,128)(2,1)S(1)}, u32[]{:S(2)}, u32[]{:S(2)}) collective-permute-start(bf16[4,512,128]{2,1,0:T(8,128)(2,1)S(1)} %get-tuple-element.81), channel_id=1, source_target_pairs={{0,8},{4,12},{8,0},{12,4},{16,24},{20,28},{24,16},{28,20},{32,40},... | collective-permute-start | bytes 1572872 | tf_op jit(solution)/shard_map/ppermute | solution.py:26
  80.4 17.5 %collective-permute-start.16 = (bf16[4,512,128]{2,1,0:T(8,128)(2,1)S(1)}, bf16[4,512,128]{2,1,0:T(8,128)(2,1)S(1)}, u32[]{:S(2)}, u32[]{:S(2)}) collective-permute-start(bf16[4,512,128]{2,1,0:T(8,128)(2,1)S(1)} %get-tuple-element.82), channel_id=1, source_target_pairs={{8,16},{12,20},{16,8},{20,12},{24,32},{28,36},{32,24},{36,28},{40,... | collective-permute-start | bytes 1572872 | tf_op jit(solution)/shard_map/ppermute | solution.py:32
  81.1 11.4 %copy-start.16 = (f32[1,640]{1,0:T(1,128)S(1)}, f32[1,640]{1,0:T(1,128)}, u32[]{:S(2)}) copy-start(f32[1,640]{1,0:T(1,128)} %stack.66) | copy-start | bytes 7684
  81.2 11.4 %copy-start.17 = (f32[1,640]{1,0:T(1,128)S(1)}, f32[1,640]{1,0:T(1,128)}, u32[]{:S(2)}) copy-start(f32[1,640]{1,0:T(1,128)} %stack.67) | copy-start | bytes 7684
  92.6 5.3 %collective-permute-start.14 = (f32[2,640]{1,0:T(2,128)S(1)}, f32[2,640]{1,0:T(2,128)S(1)}, u32[]{:S(2)}, u32[]{:S(2)}) collective-permute-start(f32[2,640]{1,0:T(2,128)S(1)} %maximum_multiply_fusion), channel_id=1, source_target_pairs={{0,4},{4,0},{8,12},{12,8},{16,20},{20,16},{24,28},{28,24},{32,36},... | collective-permute-start | bytes 15368 | tf_op jit(solution)/shard_map/ppermute | solution.py:46
  94.5 13.7 %collective-permute-start.13 = (bf16[2,512,128]{2,1,0:T(8,128)(2,1)S(1)}, bf16[2,512,128]{2,1,0:T(8,128)(2,1)S(1)}, u32[]{:S(2)}, u32[]{:S(2)}) collective-permute-start(bf16[2,512,128]{2,1,0:T(8,128)(2,1)S(1)} %get-tuple-element.75), channel_id=1, source_target_pairs={{0,4},{4,0},{8,12},{12,8},{16,20},{20,16},{24,28},{28,24},{32,36},... | collective-permute-start | bytes 786440 | tf_op jit(solution)/shard_map/ppermute | solution.py:36
  98.1 10.8 %collective-permute-start.17 = (bf16[2,512,128]{2,1,0:T(8,128)(2,1)S(1)}, bf16[2,512,128]{2,1,0:T(8,128)(2,1)S(1)}, u32[]{:S(2)}, u32[]{:S(2)}) collective-permute-start(bf16[2,512,128]{2,1,0:T(8,128)(2,1)S(1)} %get-tuple-element.87), channel_id=1, source_target_pairs={{0,4},{4,0},{8,12},{12,8},{16,20},{20,16},{24,28},{28,24},{32,36},... | collective-permute-start | bytes 786440 | tf_op jit(solution)/shard_map/ppermute | solution.py:36
  100.1 15.5 %collective-permute-start.18 = (bf16[4,512,128]{2,1,0:T(8,128)(2,1)S(1)}, bf16[4,512,128]{2,1,0:T(8,128)(2,1)S(1)}, u32[]{:S(2)}, u32[]{:S(2)}) collective-permute-start(bf16[4,512,128]{2,1,0:T(8,128)(2,1)S(1)} %get-tuple-element.91), channel_id=1, source_target_pairs={{0,8},{4,12},{8,0},{12,4},{16,24},{20,28},{24,16},{28,20},{32,40},... | collective-permute-start | bytes 1572872 | tf_op jit(solution)/shard_map/ppermute | solution.py:26
  104.4 14.9 %collective-permute-start.19 = (bf16[4,512,128]{2,1,0:T(8,128)(2,1)S(1)}, bf16[4,512,128]{2,1,0:T(8,128)(2,1)S(1)}, u32[]{:S(2)}, u32[]{:S(2)}) collective-permute-start(bf16[4,512,128]{2,1,0:T(8,128)(2,1)S(1)} %get-tuple-element.92), channel_id=1, source_target_pairs={{8,16},{12,20},{16,8},{20,12},{24,32},{28,36},{32,24},{36,28},{40,... | collective-permute-start | bytes 1572872 | tf_op jit(solution)/shard_map/ppermute | solution.py:32
  105.2 15.4 %collective-permute-start.25 = (bf16[2,512,128]{2,1,0:T(8,128)(2,1)S(1)}, bf16[2,512,128]{2,1,0:T(8,128)(2,1)S(1)}, u32[]{:S(2)}, u32[]{:S(2)}) collective-permute-start(bf16[2,512,128]{2,1,0:T(8,128)(2,1)S(1)} %add_convert_fusion.1), channel_id=1, source_target_pairs={{0,4},{4,0},{8,12},{12,8},{16,20},{20,16},{24,28},{28,24},{32,36},... | collective-permute-start | bytes 786440 | tf_op jit(solution)/shard_map/ppermute | solution.py:36
  108.2 14.8 %collective-permute-start.23 = (bf16[2,512,128]{2,1,0:T(8,128)(2,1)S(1)}, bf16[2,512,128]{2,1,0:T(8,128)(2,1)S(1)}, u32[]{:S(2)}, u32[]{:S(2)}) collective-permute-start(bf16[2,512,128]{2,1,0:T(8,128)(2,1)S(1)} %get-tuple-element.94), channel_id=1, source_target_pairs={{0,4},{4,0},{8,12},{12,8},{16,20},{20,16},{24,28},{28,24},{32,36},... | collective-permute-start | bytes 786440 | tf_op jit(solution)/shard_map/ppermute | solution.py:36
  108.9 14.2 %collective-permute-start.20 = (f32[2,640]{1,0:T(2,128)S(1)}, f32[2,640]{1,0:T(2,128)S(1)}, u32[]{:S(2)}, u32[]{:S(2)}) collective-permute-start(f32[2,640]{1,0:T(2,128)S(1)} %add.77), channel_id=1, source_target_pairs={{0,8},{4,12},{8,16},{12,20},{16,24},{20,28},{24,0},{28,4},{32,40},... | collective-permute-start | bytes 15368 | tf_op jit(solution)/shard_map/ppermute | solution.py:46
  114.6 8.0 %copy-start.7 = (bf16[2,512,640]{2,1,0:T(8,128)(2,1)}, bf16[2,512,640]{2,1,0:T(8,128)(2,1)S(1)}, u32[]{:S(2)}) copy-start(bf16[2,512,640]{2,1,0:T(8,128)(2,1)S(1)} %pad_maximum_fusion.1) | copy-start | bytes 3932164
  115.6 7.5 %collective-permute-start.21 = (f32[2,640]{1,0:T(2,128)S(1)}, f32[2,640]{1,0:T(2,128)S(1)}, u32[]{:S(2)}, u32[]{:S(2)}) collective-permute-start(f32[2,640]{1,0:T(2,128)S(1)} %add.77), channel_id=1, source_target_pairs={{0,16},{4,20},{8,24},{12,28},{16,0},{20,4},{24,8},{28,12},{32,48},... | collective-permute-start | bytes 15368 | tf_op jit(solution)/shard_map/ppermute | solution.py:46
  119.3 3.8 %collective-permute-start.22 = (f32[2,640]{1,0:T(2,128)S(1)}, f32[2,640]{1,0:T(2,128)S(1)}, u32[]{:S(2)}, u32[]{:S(2)}) collective-permute-start(f32[2,640]{1,0:T(2,128)S(1)} %add.77), channel_id=1, source_target_pairs={{0,24},{4,28},{8,0},{12,4},{16,8},{20,12},{24,16},{28,20},{32,56},... | collective-permute-start | bytes 15368 | tf_op jit(solution)/shard_map/ppermute | solution.py:46
  120.4 2.2 %copy-start.5 = (bf16[512,640]{1,0:T(8,128)(2,1)S(1)}, bf16[512,640]{1,0:T(8,128)(2,1)}, u32[]{:S(2)}) copy-start(bf16[512,640]{1,0:T(8,128)(2,1)} %param.8) | copy-start | bytes 1966084
  120.6 8.0 %collective-permute-start.24 = (bf16[2,512,128]{2,1,0:T(8,128)(2,1)S(1)}, bf16[2,512,128]{2,1,0:T(8,128)(2,1)S(1)}, u32[]{:S(2)}, u32[]{:S(2)}) collective-permute-start(bf16[2,512,128]{2,1,0:T(8,128)(2,1)S(1)} %get-tuple-element.107), channel_id=1, source_target_pairs={{0,4},{4,0},{8,12},{12,8},{16,20},{20,16},{24,28},{28,24},{32,36},... | collective-permute-start | bytes 786440 | tf_op jit(solution)/shard_map/ppermute | solution.py:36
  128.6 16.8 %collective-permute-start.26 = (f32[2,640]{1,0:T(2,128)S(1)}, f32[2,640]{1,0:T(2,128)S(1)}, u32[]{:S(2)}, u32[]{:S(2)}) collective-permute-start(f32[2,640]{1,0:T(2,128)S(1)} %add_add_fusion.2), channel_id=1, source_target_pairs={{0,32},{4,36},{8,40},{12,44},{16,48},{20,52},{24,56},{28,60},{32,6... | collective-permute-start | bytes 15368 | tf_op jit(solution)/shard_map/ppermute | solution.py:46
  130.5 14.9 %collective-permute-start.27 = (f32[2,640]{1,0:T(2,128)S(1)}, f32[2,640]{1,0:T(2,128)S(1)}, u32[]{:S(2)}, u32[]{:S(2)}) collective-permute-start(f32[2,640]{1,0:T(2,128)S(1)} %add_add_fusion.2), channel_id=1, source_target_pairs={{0,64},{4,68},{8,72},{12,76},{16,80},{20,84},{24,88},{28,92},{32,9... | collective-permute-start | bytes 15368 | tf_op jit(solution)/shard_map/ppermute | solution.py:46
  133.4 12.0 %collective-permute-start.28 = (f32[2,640]{1,0:T(2,128)S(1)}, f32[2,640]{1,0:T(2,128)S(1)}, u32[]{:S(2)}, u32[]{:S(2)}) collective-permute-start(f32[2,640]{1,0:T(2,128)S(1)} %add_add_fusion.2), channel_id=1, source_target_pairs={{0,96},{4,100},{8,104},{12,108},{16,112},{20,116},{24,120},{28,124... | collective-permute-start | bytes 15368 | tf_op jit(solution)/shard_map/ppermute | solution.py:46
  134.2 1.1 copy-start.3
  141.5 1.2 copy-start.6
  141.5 1.8 %copy-start.8 = (bf16[2,512,640]{2,1,0:T(8,128)(2,1)S(1)}, bf16[2,512,640]{2,1,0:T(8,128)(2,1)}, u32[]{:S(2)}) copy-start(bf16[2,512,640]{2,1,0:T(8,128)(2,1)} %copy-done.7) | copy-start | bytes 3932164

commit v2 on v1

--- a/solution.py
+++ b/solution.py
@@ -56,7 +56,7 @@
 
 
 STEPS = 4 + ROUNDS
-DIRECT = 2
+DIRECT = 1
 INT_COUNT = STEPS * 4
 BIAS_CENTRE = STEPS * 4
 

time: 146 us -> 146 us (level)
    ppermute x7, starting transfers between devices: 17.4 us -> 15.6 us  [summed_over_digit(): parts.append(lax.ppermute(value, 'tm', pairs))]
  transfers between devices with their start and end apart: 29 -> 29, of which waited for: 4 -> 4; matrix products, arithmetic and copies ran while one was open for 11% -> 12% of each run, Pallas kernels for 22% -> 22%
where the time goes in v2:
time: 146 us; the launch traced here: 145 us
  starting transfers between devices  66.6 us (46%)
  Pallas kernels  32.5 us (22%)
  blocking collectives  12.7 us (9%)
  other arithmetic  12.6 us (9%)
  local copies, waits for them, and re-layouts  10.2 us (7%)
  waiting for transfers between devices  8.89 us (6%)
    pallas_call x3, Pallas kernels, attention_slot(): pl.pallas_call(functools.partial(attention_kernel, groups_here), grid=(1,...  28.8 us
    ppermute x7, starting transfers between devices, to_near(): lax.ppermute(value, axis, [(s, s ^ 2) for s in range(lax.axis_size(axis))])  28.5 us
    ppermute x8, starting transfers between devices, swapped(): lax.ppermute(value, axis, [(s, s ^ 1) for s in range(lax.axis_size(axis))])  16.1 us
    ppermute x7, starting transfers between devices, summed_over_digit(): parts.append(lax.ppermute(value, 'tm', pairs))  15.6 us
    ppermute x8, waiting for transfers between devices, swapped(): lax.ppermute(value, axis, [(s, s ^ 1) for s in range(lax.axis_size(axis))])  7.33 us
    psum x1, blocking collectives, shards(): squares = lax.psum(shares, 'head')  7.07 us
    ppermute x7, starting transfers between devices, to_far(): lax.ppermute(value, axis, [(s, d) for s, d in pairs if 0 <= d < count])  6.37 us
    psum x1, blocking collectives, shards(): lax.psum(jnp.stack([jnp.sum(query_back * query_unit, axis=1), jnp.sum(key...  5.67 us
  transfers between devices with their start and end apart: 29, of which 4 were waited for; matrix products, arithmetic and copies ran while one was open for 12% of the time, Pallas kernels for 22%

profile of v2, /device:TPU:0, one launch (start us, length us, event | category | flops | bytes accessed | tf_op | source)
XLA Modules:
  0.0 144.7 jit_solution(1524058824029572037)
XLA Ops:
  0.7 1.4 fusion.17
  2.1 1.3 fusion.11
  3.4 7.1 %psum.14 = f32[2,512]{1,0:T(2,128)S(1)} all-reduce(f32[2,512]{1,0:T(2,128)S(1)} %pad_maximum_fusion.10), channel_id=1, replica_groups=mesh['tm'=32,'head'=4] {'head'}, use_global_device_ids=true, to_apply=%region_2.3 | all-reduce | flops 1024 | bytes 8192 | tf_op jit(solution)/shard_map/psum | solution.py:514
  10.8 0.8 slice-done
  11.7 2.0 %collective-permute-start.1 = (bf16[512,384]{1,0:T(8,128)(2,1)S(1)}, bf16[512,384]{1,0:T(8,128)(2,1)S(1)}, u32[]{:S(2)}, u32[]{:S(2)}) collective-permute-start(bf16[512,384]{1,0:T(8,128)(2,1)S(1)} %get-tuple-element.63.own_value), channel_id=1, source_target_pairs={{0,8},{4,12},{8,0},{12,4},{16,24},{20,28},{24,16},{28,20},{32,40},... | collective-permute-start | bytes 1179656 | tf_op jit(solution)/shard_map/ppermute | solution.py:26
  14.5 3.0 %collective-permute-start = (bf16[512,384]{1,0:T(8,128)(2,1)S(1)}, bf16[512,384]{1,0:T(8,128)(2,1)S(1)}, u32[]{:S(2)}, u32[]{:S(2)}) collective-permute-start(bf16[512,384]{1,0:T(8,128)(2,1)S(1)} %get-tuple-element.122), channel_id=1, source_target_pairs={{0,4},{4,0},{8,12},{12,8},{16,20},{20,16},{24,28},{28,24},{32,36},... | collective-permute-start | bytes 1179656 | tf_op jit(solution)/shard_map/ppermute | solution.py:36
  18.1 4.8 %collective-permute-start.4 = (bf16[512,384]{1,0:T(8,128)(2,1)S(1)}, bf16[512,384]{1,0:T(8,128)(2,1)S(1)}, u32[]{:S(2)}, u32[]{:S(2)}) collective-permute-start(bf16[512,384]{1,0:T(8,128)(2,1)S(1)} %get-tuple-element.57.own_key), channel_id=1, source_target_pairs={{0,8},{4,12},{8,0},{12,4},{16,24},{20,28},{24,16},{28,20},{32,40},... | collective-permute-start | bytes 1179656 | tf_op jit(solution)/shard_map/ppermute | solution.py:26
  23.7 0.9 select_bitcast_fusion.3
  24.6 0.8 select_bitcast_fusion
  26.8 1.4 collective-permute-done.partner_key
  28.1 4.8 %collective-permute-start.5 = (bf16[512,384]{1,0:T(8,128)(2,1)S(1)}, bf16[512,384]{1,0:T(8,128)(2,1)S(1)}, u32[]{:S(2)}, u32[]{:S(2)}) collective-permute-start(bf16[512,384]{1,0:T(8,128)(2,1)S(1)} %collective-permute-done.partner_key), channel_id=1, source_target_pairs={{0,8},{4,12},{8,0},{12,4},{16,24},{20,28},{24,16},{28,20},{32,40},... | collective-permute-start | bytes 1179656 | tf_op jit(solution)/shard_map/ppermute | solution.py:26
  32.9 1.4 collective-permute-start.7
  34.3 1.4 collective-permute-start.10
  35.7 4.9 %collective-permute-start.9 = (bf16[512,384]{1,0:T(8,128)(2,1)S(1)}, bf16[512,384]{1,0:T(8,128)(2,1)}, u32[]{:S(2)}, u32[]{:S(2)}) collective-permute-start(bf16[512,384]{1,0:T(8,128)(2,1)S(1)} %collective-permute-done.8.partner_value), channel_id=1, source_target_pairs={{0,8},{4,12},{8,0},{12,4},{16,24},{20,28},{24,16},{28,20},{32,40},... | collective-permute-start | bytes 1179656 | tf_op jit(solution)/shard_map/ppermute | solution.py:26
  41.2 1.4 copy.14.mask
  42.7 1.3 stack.66
  43.9 1.3 stack.67
  45.2 3.7 %live_tables.1 = (s32[2,65]{1,0:T(2,128)}, f32[2,80]{1,0:T(2,128)}) custom-call(s32[2]{0:T(128)} %pad_add_fusion.chain, s32[128,20]{1,0:T(8,128)} %copy.14.mask, s32[3]{0:T(128)} %strides.1), custom_call_target="tpu_custom_call" | custom-call | tf_op jit(solution)/shard_map/live_tables/pallas_call | solution.py:135
  48.9 1.1 pad_maximum_fusion.3
  50.0 3.3 %collective-permute-start.3 = (bf16[2,512,256]{2,1,0:T(8,128)(2,1)S(1)}, bf16[2,512,256]{2,1,0:T(8,128)(2,1)S(1)}, u32[]{:S(2)}, u32[]{:S(2)}) collective-permute-start(bf16[2,512,256]{2,1,0:T(8,128)(2,1)S(1)} %pad_maximum_fusion.3), channel_id=1, source_target_pairs={{0,4},{4,0},{8,12},{12,8},{16,20},{20,16},{24,28},{28,24},{32,36},... | collective-permute-start | bytes 1572872 | tf_op jit(solution)/shard_map/ppermute | solution.py:36
  53.3 1.0 slice_bitcast_fusion.3
  54.4 6.1 %attention_slot.4 = (bf16[2,512,128]{2,1,0:T(8,128)(2,1)S(1)}, bf16[2,512,128]{2,1,0:T(8,128)(2,1)}, bf16[4,512,128]{2,1,0:T(8,128)(2,1)S(1)}, bf16[4,512,128]{2...) custom-call(s32[2,65]{1,0:T(2,128)S(1)} %copy-done, f32[2,80]{1,0:T(2,128)S(1)} %copy-done.1, ...), custom_call_target="tpu_custom_call" | custom-call | flops 4026531840 | bytes 6291456 | tf_op jit(solution)/shard_map/attention_slot/pallas_call | solution.py:435
  60.4 0.8 collective-permute-start.11
  61.3 0.9 collective-permute-start.12
  62.7 11.3 %attention_slot.3 = (bf16[2,512,128]{2,1,0:T(8,128)(2,1)S(1)}, bf16[2,512,128]{2,1,0:T(8,128)(2,1)S(1)}, bf16[4,512,128]{2,1,0:T(8,128)(2,1)S(1)}, bf16[4,512,12...) custom-call(s32[2,65]{1,0:T(2,128)S(1)} %copy-done, f32[2,80]{1,0:T(2,128)S(1)} %copy-done.1, ...), custom_call_target="tpu_custom_call" | custom-call | flops 8053063680 | bytes 6291456 | tf_op jit(solution)/shard_map/attention_slot/pallas_call | solution.py:435
  74.0 6.1 %collective-permute-start.15 = (bf16[4,512,128]{2,1,0:T(8,128)(2,1)S(1)}, bf16[4,512,128]{2,1,0:T(8,128)(2,1)S(1)}, u32[]{:S(2)}, u32[]{:S(2)}) collective-permute-start(bf16[4,512,128]{2,1,0:T(8,128)(2,1)S(1)} %get-tuple-element.81), channel_id=1, source_target_pairs={{0,8},{4,12},{8,0},{12,4},{16,24},{20,28},{24,16},{28,20},{32,40},... | collective-permute-start | bytes 1572872 | tf_op jit(solution)/shard_map/ppermute | solution.py:26
  80.8 11.4 %attention_slot.5 = (bf16[2,512,128]{2,1,0:T(8,128)(2,1)S(1)}, bf16[2,512,128]{2,1,0:T(8,128)(2,1)S(1)}, bf16[4,512,128]{2,1,0:T(8,128)(2,1)S(1)}, bf16[4,512,12...) custom-call(s32[2,65]{1,0:T(2,128)S(1)} %copy-done, f32[2,80]{1,0:T(2,128)S(1)} %copy-done.1, ...), custom_call_target="tpu_custom_call" | custom-call | flops 8053063680 | bytes 6291456 | tf_op jit(solution)/shard_map/attention_slot/pallas_call | solution.py:435
  92.3 1.9 %collective-permute-start.14 = (f32[2,640]{1,0:T(2,128)S(1)}, f32[2,640]{1,0:T(2,128)S(1)}, u32[]{:S(2)}, u32[]{:S(2)}) collective-permute-start(f32[2,640]{1,0:T(2,128)S(1)} %maximum_multiply_fusion), channel_id=1, source_target_pairs={{0,4},{4,0},{8,12},{12,8},{16,20},{20,16},{24,28},{28,24},{32,36},... | collective-permute-start | bytes 15368 | tf_op jit(solution)/shard_map/ppermute | solution.py:46
  94.3 1.7 %collective-permute-start.13 = (bf16[2,512,128]{2,1,0:T(8,128)(2,1)S(1)}, bf16[2,512,128]{2,1,0:T(8,128)(2,1)S(1)}, u32[]{:S(2)}, u32[]{:S(2)}) collective-permute-start(bf16[2,512,128]{2,1,0:T(8,128)(2,1)S(1)} %get-tuple-element.75), channel_id=1, source_target_pairs={{0,4},{4,0},{8,12},{12,8},{16,20},{20,16},{24,28},{28,24},{32,36},... | collective-permute-start | bytes 786440 | tf_op jit(solution)/shard_map/ppermute | solution.py:36
  96.0 1.5 %collective-permute-done.14 = f32[2,640]{1,0:T(2,128)S(1)} collective-permute-done((f32[2,640]{1,0:T(2,128)S(1)}, f32[2,640]{1,0:T(2,128)S(1)}, u32[]{:S(2)}, u32[]{:S(2)}) %collective-permute-start.14) | collective-permute-done | bytes 5152 | tf_op jit(solution)/shard_map/ppermute | solution.py:46
  97.8 2.2 %collective-permute-start.17 = (bf16[2,512,128]{2,1,0:T(8,128)(2,1)S(1)}, bf16[2,512,128]{2,1,0:T(8,128)(2,1)S(1)}, u32[]{:S(2)}, u32[]{:S(2)}) collective-permute-start(bf16[2,512,128]{2,1,0:T(8,128)(2,1)S(1)} %get-tuple-element.87), channel_id=1, source_target_pairs={{0,4},{4,0},{8,12},{12,8},{16,20},{20,16},{24,28},{28,24},{32,36},... | collective-permute-start | bytes 786440 | tf_op jit(solution)/shard_map/ppermute | solution.py:36
  100.0 5.1 %collective-permute-start.18 = (bf16[4,512,128]{2,1,0:T(8,128)(2,1)S(1)}, bf16[4,512,128]{2,1,0:T(8,128)(2,1)S(1)}, u32[]{:S(2)}, u32[]{:S(2)}) collective-permute-start(bf16[4,512,128]{2,1,0:T(8,128)(2,1)S(1)} %get-tuple-element.91), channel_id=1, source_target_pairs={{0,8},{4,12},{8,0},{12,4},{16,24},{20,28},{24,16},{28,20},{32,40},... | collective-permute-start | bytes 1572872 | tf_op jit(solution)/shard_map/ppermute | solution.py:26
  105.9 2.3 %collective-permute-start.25 = (bf16[2,512,128]{2,1,0:T(8,128)(2,1)S(1)}, bf16[2,512,128]{2,1,0:T(8,128)(2,1)S(1)}, u32[]{:S(2)}, u32[]{:S(2)}) collective-permute-start(bf16[2,512,128]{2,1,0:T(8,128)(2,1)S(1)} %add_convert_fusion.1), channel_id=1, source_target_pairs={{0,4},{4,0},{8,12},{12,8},{16,20},{20,16},{24,28},{28,24},{32,36},... | collective-permute-start | bytes 786440 | tf_op jit(solution)/shard_map/ppermute | solution.py:36
  108.1 1.3 collective-permute-start.23
  109.5 4.8 %collective-permute-start.20 = (f32[2,640]{1,0:T(2,128)S(1)}, f32[2,640]{1,0:T(2,128)S(1)}, u32[]{:S(2)}, u32[]{:S(2)}) collective-permute-start(f32[2,640]{1,0:T(2,128)S(1)} %add.77), channel_id=1, source_target_pairs={{0,8},{4,12},{8,16},{12,20},{16,24},{20,28},{24,0},{28,4},{32,40},... | collective-permute-start | bytes 15368 | tf_op jit(solution)/shard_map/ppermute | solution.py:46
  114.6 1.0 slice_bitcast_fusion.2
  115.6 2.0 %collective-permute-start.21 = (f32[2,640]{1,0:T(2,128)S(1)}, f32[2,640]{1,0:T(2,128)S(1)}, u32[]{:S(2)}, u32[]{:S(2)}) collective-permute-start(f32[2,640]{1,0:T(2,128)S(1)} %add.77), channel_id=1, source_target_pairs={{0,16},{4,20},{8,24},{12,28},{16,0},{20,4},{24,8},{28,12},{32,48},... | collective-permute-start | bytes 15368 | tf_op jit(solution)/shard_map/ppermute | solution.py:46
  117.7 1.8 %collective-permute-start.22 = (f32[2,640]{1,0:T(2,128)S(1)}, f32[2,640]{1,0:T(2,128)S(1)}, u32[]{:S(2)}, u32[]{:S(2)}) collective-permute-start(f32[2,640]{1,0:T(2,128)S(1)} %add.77), channel_id=1, source_target_pairs={{0,24},{4,28},{8,0},{12,4},{16,8},{20,12},{24,16},{28,20},{32,56},... | collective-permute-start | bytes 15368 | tf_op jit(solution)/shard_map/ppermute | solution.py:46
  119.7 1.8 %collective-permute-start.24 = (bf16[2,512,128]{2,1,0:T(8,128)(2,1)S(1)}, bf16[2,512,128]{2,1,0:T(8,128)(2,1)S(1)}, u32[]{:S(2)}, u32[]{:S(2)}) collective-permute-start(bf16[2,512,128]{2,1,0:T(8,128)(2,1)S(1)} %get-tuple-element.107), channel_id=1, source_target_pairs={{0,4},{4,0},{8,12},{12,8},{16,20},{20,16},{24,28},{28,24},{32,36},... | collective-permute-start | bytes 786440 | tf_op jit(solution)/shard_map/ppermute | solution.py:36
  122.1 5.6 %collective-permute-done.24 = bf16[2,512,128]{2,1,0:T(8,128)(2,1)S(1)} collective-permute-done((bf16[2,512,128]{2,1,0:T(8,128)(2,1)S(1)}, bf16[2,512,128]{2,1,0:T(8,128)(2,1)S(1)}, u32[]{:S(2)}, u32[]{:S(2)}) %collective-permute-start.24) | collective-permute-done | bytes 262176 | tf_op jit(solution)/shard_map/ppermute | solution.py:36
  127.7 1.9 %collective-permute-start.26 = (f32[2,640]{1,0:T(2,128)S(1)}, f32[2,640]{1,0:T(2,128)S(1)}, u32[]{:S(2)}, u32[]{:S(2)}) collective-permute-start(f32[2,640]{1,0:T(2,128)S(1)} %add_add_fusion.2), channel_id=1, source_target_pairs={{0,32},{4,36},{8,40},{12,44},{16,48},{20,52},{24,56},{28,60},{32,6... | collective-permute-start | bytes 15368 | tf_op jit(solution)/shard_map/ppermute | solution.py:46
  129.6 1.7 %collective-permute-start.27 = (f32[2,640]{1,0:T(2,128)S(1)}, f32[2,640]{1,0:T(2,128)S(1)}, u32[]{:S(2)}, u32[]{:S(2)}) collective-permute-start(f32[2,640]{1,0:T(2,128)S(1)} %add_add_fusion.2), channel_id=1, source_target_pairs={{0,64},{4,68},{8,72},{12,76},{16,80},{20,84},{24,88},{28,92},{32,9... | collective-permute-start | bytes 15368 | tf_op jit(solution)/shard_map/ppermute | solution.py:46
  131.3 1.4 collective-permute-start.28
  133.2 0.9 copy-done.3
  134.5 5.7 %psum.15 = f32[2,512]{1,0:T(2,128)S(1)} all-reduce(f32[2,512]{1,0:T(2,128)S(1)} %pad_maximum_fusion.11), channel_id=1, replica_groups=mesh['tm'=32,'head'=4] {'head'}, use_global_device_ids=true, to_apply=%region_5.6 | all-reduce | flops 1024 | bytes 8192 | tf_op jit(solution)/shard_map/psum | solution.py:604
  140.2 1.2 fusion.16
  141.9 1.2 fusion.10
  143.1 0.9 fusion.21
  (112 shorter events, 10.1 us)
Async XLA Ops:
  0.6 9.8 %copy-start.2 = (bf16[512,640]{1,0:T(8,128)(2,1)S(1)}, bf16[512,640]{1,0:T(8,128)(2,1)}, u32[]{:S(2)}) copy-start(bf16[512,640]{1,0:T(8,128)(2,1)} %param.9) | copy-start | bytes 1966084
  0.6 9.8 %copy-start.14 = (f32[640]{0:T(1024)S(1)}, f32[640]{0:T(1024)}, u32[]{:S(2)}) copy-start(f32[640]{0:T(1024)} %param.12) | copy-start | bytes 7684
  0.7 10.0 %copy-start.12 = (bf16[512,640]{1,0:T(8,128)(2,1)S(1)}, bf16[512,640]{1,0:T(8,128)(2,1)}, u32[]{:S(2)}) copy-start(bf16[512,640]{1,0:T(8,128)(2,1)} %param.10) | copy-start | bytes 1966084
  10.7 0.9 slice-start
  11.6 11.2 %copy-start.15 = (f32[640]{0:T(1024)S(1)}, f32[640]{0:T(1024)}, u32[]{:S(2)}) copy-start(f32[640]{0:T(1024)} %param.11) | copy-start | bytes 7684
  11.6 11.8 %copy-start.4 = (bf16[512,640]{1,0:T(8,128)(2,1)S(1)}, bf16[512,640]{1,0:T(8,128)(2,1)}, u32[]{:S(2)}) copy-start(bf16[512,640]{1,0:T(8,128)(2,1)} %param.8) | copy-start | bytes 1966084
  11.7 13.8 %collective-permute-start.1 = (bf16[512,384]{1,0:T(8,128)(2,1)S(1)}, bf16[512,384]{1,0:T(8,128)(2,1)S(1)}, u32[]{:S(2)}, u32[]{:S(2)}) collective-permute-start(bf16[512,384]{1,0:T(8,128)(2,1)S(1)} %get-tuple-element.63.own_value), channel_id=1, source_target_pairs={{0,8},{4,12},{8,0},{12,4},{16,24},{20,28},{24,16},{28,20},{32,40},... | collective-permute-start | bytes 1179656 | tf_op jit(solution)/shard_map/ppermute | solution.py:26
  13.7 13.0 %collective-permute-start.2 = (bf16[512,384]{1,0:T(8,128)(2,1)S(1)}, bf16[512,384]{1,0:T(8,128)(2,1)S(1)}, u32[]{:S(2)}, u32[]{:S(2)}) collective-permute-start(bf16[512,384]{1,0:T(8,128)(2,1)S(1)} %get-tuple-element.63.own_value), channel_id=1, source_target_pairs={{8,16},{12,20},{16,8},{20,12},{24,32},{28,36},{32,24},{36,28},{40,... | collective-permute-start | bytes 1179656 | tf_op jit(solution)/shard_map/ppermute | solution.py:32
  14.5 10.1 %copy-start.13 = (bf16[512,640]{1,0:T(8,128)(2,1)S(1)}, bf16[512,640]{1,0:T(8,128)(2,1)}, u32[]{:S(2)}) copy-start(bf16[512,640]{1,0:T(8,128)(2,1)} %param.13) | copy-start | bytes 1966084
  14.5 13.6 %collective-permute-start = (bf16[512,384]{1,0:T(8,128)(2,1)S(1)}, bf16[512,384]{1,0:T(8,128)(2,1)S(1)}, u32[]{:S(2)}, u32[]{:S(2)}) collective-permute-start(bf16[512,384]{1,0:T(8,128)(2,1)S(1)} %get-tuple-element.122), channel_id=1, source_target_pairs={{0,4},{4,0},{8,12},{12,8},{16,20},{20,16},{24,28},{28,24},{32,36},... | collective-permute-start | bytes 1179656 | tf_op jit(solution)/shard_map/ppermute | solution.py:36
  17.5 16.8 %collective-permute-start.8 = (bf16[512,384]{1,0:T(8,128)(2,1)S(1)}, bf16[512,384]{1,0:T(8,128)(2,1)S(1)}, u32[]{:S(2)}, u32[]{:S(2)}) collective-permute-start(bf16[512,384]{1,0:T(8,128)(2,1)S(1)} %get-tuple-element.120), channel_id=1, source_target_pairs={{0,4},{4,0},{8,12},{12,8},{16,20},{20,16},{24,28},{28,24},{32,36},... | collective-permute-start | bytes 1179656 | tf_op jit(solution)/shard_map/ppermute | solution.py:36
  18.1 17.6 %collective-permute-start.4 = (bf16[512,384]{1,0:T(8,128)(2,1)S(1)}, bf16[512,384]{1,0:T(8,128)(2,1)S(1)}, u32[]{:S(2)}, u32[]{:S(2)}) collective-permute-start(bf16[512,384]{1,0:T(8,128)(2,1)S(1)} %get-tuple-element.57.own_key), channel_id=1, source_target_pairs={{0,8},{4,12},{8,0},{12,4},{16,24},{20,28},{24,16},{28,20},{32,40},... | collective-permute-start | bytes 1179656 | tf_op jit(solution)/shard_map/ppermute | solution.py:26
  23.7 12.0 %copy-start.9 = (bf16[512,640]{1,0:T(8,128)(2,1)}, bf16[512,640]{1,0:T(8,128)(2,1)S(1)}, u32[]{:S(2)}) copy-start(bf16[512,640]{1,0:T(8,128)(2,1)S(1)} %fusion.6) | copy-start | bytes 1966084
  25.5 24.5 %collective-permute-start.6 = (bf16[512,384]{1,0:T(8,128)(2,1)S(1)}, bf16[512,384]{1,0:T(8,128)(2,1)S(1)}, u32[]{:S(2)}, u32[]{:S(2)}) collective-permute-start(bf16[512,384]{1,0:T(8,128)(2,1)S(1)} %get-tuple-element.57.own_key), channel_id=1, source_target_pairs={{8,16},{12,20},{16,8},{20,12},{24,32},{28,36},{32,24},{36,28},{40,... | collective-permute-start | bytes 1179656 | tf_op jit(solution)/shard_map/ppermute | solution.py:32
  28.1 26.2 %collective-permute-start.5 = (bf16[512,384]{1,0:T(8,128)(2,1)S(1)}, bf16[512,384]{1,0:T(8,128)(2,1)S(1)}, u32[]{:S(2)}, u32[]{:S(2)}) collective-permute-start(bf16[512,384]{1,0:T(8,128)(2,1)S(1)} %collective-permute-done.partner_key), channel_id=1, source_target_pairs={{0,8},{4,12},{8,0},{12,4},{16,24},{20,28},{24,16},{28,20},{32,40},... | collective-permute-start | bytes 1179656 | tf_op jit(solution)/shard_map/ppermute | solution.py:26
  32.9 21.4 %collective-permute-start.7 = (bf16[512,384]{1,0:T(8,128)(2,1)S(1)}, bf16[512,384]{1,0:T(8,128)(2,1)}, u32[]{:S(2)}, u32[]{:S(2)}) collective-permute-start(bf16[512,384]{1,0:T(8,128)(2,1)S(1)} %collective-permute-done.partner_key), channel_id=1, source_target_pairs={{8,16},{12,20},{16,8},{20,12},{24,32},{28,36},{32,24},{36,28},{40,... | collective-permute-start | bytes 1179656 | tf_op jit(solution)/shard_map/ppermute | solution.py:32
  34.3 20.0 %collective-permute-start.10 = (bf16[512,384]{1,0:T(8,128)(2,1)S(1)}, bf16[512,384]{1,0:T(8,128)(2,1)}, u32[]{:S(2)}, u32[]{:S(2)}) collective-permute-start(bf16[512,384]{1,0:T(8,128)(2,1)S(1)} %collective-permute-done.8.partner_value), channel_id=1, source_target_pairs={{8,16},{12,20},{16,8},{20,12},{24,32},{28,36},{32,24},{36,28},{40,... | collective-permute-start | bytes 1179656 | tf_op jit(solution)/shard_map/ppermute | solution.py:32
  35.7 18.6 %collective-permute-start.9 = (bf16[512,384]{1,0:T(8,128)(2,1)S(1)}, bf16[512,384]{1,0:T(8,128)(2,1)}, u32[]{:S(2)}, u32[]{:S(2)}) collective-permute-start(bf16[512,384]{1,0:T(8,128)(2,1)S(1)} %collective-permute-done.8.partner_value), channel_id=1, source_target_pairs={{0,8},{4,12},{8,0},{12,4},{16,24},{20,28},{24,16},{28,20},{32,40},... | collective-permute-start | bytes 1179656 | tf_op jit(solution)/shard_map/ppermute | solution.py:26
  48.9 5.5 %copy-start = (s32[2,65]{1,0:T(2,128)S(1)}, s32[2,65]{1,0:T(2,128)}, u32[]{:S(2)}) copy-start(s32[2,65]{1,0:T(2,128)} %get-tuple-element.53.ints) | copy-start | bytes 1564
  48.9 5.4 %copy-start.1 = (f32[2,80]{1,0:T(2,128)S(1)}, f32[2,80]{1,0:T(2,128)}, u32[]{:S(2)}) copy-start(f32[2,80]{1,0:T(2,128)} %get-tuple-element.54.bias) | copy-start | bytes 1924
  50.0 12.5 %collective-permute-start.3 = (bf16[2,512,256]{2,1,0:T(8,128)(2,1)S(1)}, bf16[2,512,256]{2,1,0:T(8,128)(2,1)S(1)}, u32[]{:S(2)}, u32[]{:S(2)}) collective-permute-start(bf16[2,512,256]{2,1,0:T(8,128)(2,1)S(1)} %pad_maximum_fusion.3), channel_id=1, source_target_pairs={{0,4},{4,0},{8,12},{12,8},{16,20},{20,16},{24,28},{28,24},{32,36},... | collective-permute-start | bytes 1572872 | tf_op jit(solution)/shard_map/ppermute | solution.py:36
  54.4 8.2 %copy-start.11 = (bf16[1,512,256]{2,1,0:T(8,128)(2,1)S(1)}, bf16[1,512,256]{2,1,0:T(8,128)(2,1)}, u32[]{:S(2)}) copy-start(bf16[1,512,256]{2,1,0:T(8,128)(2,1)} %get-tuple-element.112) | copy-start | bytes 786436
  60.4 2.2 %copy-start.10 = (bf16[1,512,256]{2,1,0:T(8,128)(2,1)S(1)}, bf16[1,512,256]{2,1,0:T(8,128)(2,1)}, u32[]{:S(2)}) copy-start(bf16[1,512,256]{2,1,0:T(8,128)(2,1)} %get-tuple-element.110) | copy-start | bytes 786436
  60.4 20.4 %collective-permute-start.11 = (bf16[4,512,128]{2,1,0:T(8,128)(2,1)S(1)}, bf16[4,512,128]{2,1,0:T(8,128)(2,1)S(1)}, u32[]{:S(2)}, u32[]{:S(2)}) collective-permute-start(bf16[4,512,128]{2,1,0:T(8,128)(2,1)S(1)} %get-tuple-element.71), channel_id=1, source_target_pairs={{0,8},{4,12},{8,0},{12,4},{16,24},{20,28},{24,16},{28,20},{32,40},... | collective-permute-start | bytes 1572872 | tf_op jit(solution)/shard_map/ppermute | solution.py:26
  61.3 19.5 %collective-permute-start.12 = (bf16[4,512,128]{2,1,0:T(8,128)(2,1)S(1)}, bf16[4,512,128]{2,1,0:T(8,128)(2,1)S(1)}, u32[]{:S(2)}, u32[]{:S(2)}) collective-permute-start(bf16[4,512,128]{2,1,0:T(8,128)(2,1)S(1)} %get-tuple-element.72), channel_id=1, source_target_pairs={{8,16},{12,20},{16,8},{20,12},{24,32},{28,36},{32,24},{36,28},{40,... | collective-permute-start | bytes 1572872 | tf_op jit(solution)/shard_map/ppermute | solution.py:32
  74.0 23.6 %collective-permute-start.15 = (bf16[4,512,128]{2,1,0:T(8,128)(2,1)S(1)}, bf16[4,512,128]{2,1,0:T(8,128)(2,1)S(1)}, u32[]{:S(2)}, u32[]{:S(2)}) collective-permute-start(bf16[4,512,128]{2,1,0:T(8,128)(2,1)S(1)} %get-tuple-element.81), channel_id=1, source_target_pairs={{0,8},{4,12},{8,0},{12,4},{16,24},{20,28},{24,16},{28,20},{32,40},... | collective-permute-start | bytes 1572872 | tf_op jit(solution)/shard_map/ppermute | solution.py:26
  80.1 17.5 %collective-permute-start.16 = (bf16[4,512,128]{2,1,0:T(8,128)(2,1)S(1)}, bf16[4,512,128]{2,1,0:T(8,128)(2,1)S(1)}, u32[]{:S(2)}, u32[]{:S(2)}) collective-permute-start(bf16[4,512,128]{2,1,0:T(8,128)(2,1)S(1)} %get-tuple-element.82), channel_id=1, source_target_pairs={{8,16},{12,20},{16,8},{20,12},{24,32},{28,36},{32,24},{36,28},{40,... | collective-permute-start | bytes 1572872 | tf_op jit(solution)/shard_map/ppermute | solution.py:32
  80.8 11.5 %copy-start.16 = (f32[1,640]{1,0:T(1,128)S(1)}, f32[1,640]{1,0:T(1,128)}, u32[]{:S(2)}) copy-start(f32[1,640]{1,0:T(1,128)} %stack.66) | copy-start | bytes 7684
  80.8 11.5 %copy-start.17 = (f32[1,640]{1,0:T(1,128)S(1)}, f32[1,640]{1,0:T(1,128)}, u32[]{:S(2)}) copy-start(f32[1,640]{1,0:T(1,128)} %stack.67) | copy-start | bytes 7684
  92.3 5.2 %collective-permute-start.14 = (f32[2,640]{1,0:T(2,128)S(1)}, f32[2,640]{1,0:T(2,128)S(1)}, u32[]{:S(2)}, u32[]{:S(2)}) collective-permute-start(f32[2,640]{1,0:T(2,128)S(1)} %maximum_multiply_fusion), channel_id=1, source_target_pairs={{0,4},{4,0},{8,12},{12,8},{16,20},{20,16},{24,28},{28,24},{32,36},... | collective-permute-start | bytes 15368 | tf_op jit(solution)/shard_map/ppermute | solution.py:46
  94.3 13.9 %collective-permute-start.13 = (bf16[2,512,128]{2,1,0:T(8,128)(2,1)S(1)}, bf16[2,512,128]{2,1,0:T(8,128)(2,1)S(1)}, u32[]{:S(2)}, u32[]{:S(2)}) collective-permute-start(bf16[2,512,128]{2,1,0:T(8,128)(2,1)S(1)} %get-tuple-element.75), channel_id=1, source_target_pairs={{0,4},{4,0},{8,12},{12,8},{16,20},{20,16},{24,28},{28,24},{32,36},... | collective-permute-start | bytes 786440 | tf_op jit(solution)/shard_map/ppermute | solution.py:36
  97.8 11.8 %collective-permute-start.17 = (bf16[2,512,128]{2,1,0:T(8,128)(2,1)S(1)}, bf16[2,512,128]{2,1,0:T(8,128)(2,1)S(1)}, u32[]{:S(2)}, u32[]{:S(2)}) collective-permute-start(bf16[2,512,128]{2,1,0:T(8,128)(2,1)S(1)} %get-tuple-element.87), channel_id=1, source_target_pairs={{0,4},{4,0},{8,12},{12,8},{16,20},{20,16},{24,28},{28,24},{32,36},... | collective-permute-start | bytes 786440 | tf_op jit(solution)/shard_map/ppermute | solution.py:36
  100.0 15.6 %collective-permute-start.18 = (bf16[4,512,128]{2,1,0:T(8,128)(2,1)S(1)}, bf16[4,512,128]{2,1,0:T(8,128)(2,1)S(1)}, u32[]{:S(2)}, u32[]{:S(2)}) collective-permute-start(bf16[4,512,128]{2,1,0:T(8,128)(2,1)S(1)} %get-tuple-element.91), channel_id=1, source_target_pairs={{0,8},{4,12},{8,0},{12,4},{16,24},{20,28},{24,16},{28,20},{32,40},... | collective-permute-start | bytes 1572872 | tf_op jit(solution)/shard_map/ppermute | solution.py:26
  105.1 12.6 %collective-permute-start.19 = (bf16[4,512,128]{2,1,0:T(8,128)(2,1)S(1)}, bf16[4,512,128]{2,1,0:T(8,128)(2,1)S(1)}, u32[]{:S(2)}, u32[]{:S(2)}) collective-permute-start(bf16[4,512,128]{2,1,0:T(8,128)(2,1)S(1)} %get-tuple-element.92), channel_id=1, source_target_pairs={{8,16},{12,20},{16,8},{20,12},{24,32},{28,36},{32,24},{36,28},{40,... | collective-permute-start | bytes 1572872 | tf_op jit(solution)/shard_map/ppermute | solution.py:32
  105.9 13.8 %collective-permute-start.25 = (bf16[2,512,128]{2,1,0:T(8,128)(2,1)S(1)}, bf16[2,512,128]{2,1,0:T(8,128)(2,1)S(1)}, u32[]{:S(2)}, u32[]{:S(2)}) collective-permute-start(bf16[2,512,128]{2,1,0:T(8,128)(2,1)S(1)} %add_convert_fusion.1), channel_id=1, source_target_pairs={{0,4},{4,0},{8,12},{12,8},{16,20},{20,16},{24,28},{28,24},{32,36},... | collective-permute-start | bytes 786440 | tf_op jit(solution)/shard_map/ppermute | solution.py:36
  108.1 13.8 %collective-permute-start.23 = (bf16[2,512,128]{2,1,0:T(8,128)(2,1)S(1)}, bf16[2,512,128]{2,1,0:T(8,128)(2,1)S(1)}, u32[]{:S(2)}, u32[]{:S(2)}) collective-permute-start(bf16[2,512,128]{2,1,0:T(8,128)(2,1)S(1)} %get-tuple-element.94), channel_id=1, source_target_pairs={{0,4},{4,0},{8,12},{12,8},{16,20},{20,16},{24,28},{28,24},{32,36},... | collective-permute-start | bytes 786440 | tf_op jit(solution)/shard_map/ppermute | solution.py:36
  109.5 12.5 %collective-permute-start.20 = (f32[2,640]{1,0:T(2,128)S(1)}, f32[2,640]{1,0:T(2,128)S(1)}, u32[]{:S(2)}, u32[]{:S(2)}) collective-permute-start(f32[2,640]{1,0:T(2,128)S(1)} %add.77), channel_id=1, source_target_pairs={{0,8},{4,12},{8,16},{12,20},{16,24},{20,28},{24,0},{28,4},{32,40},... | collective-permute-start | bytes 15368 | tf_op jit(solution)/shard_map/ppermute | solution.py:46
  114.6 6.8 %copy-start.7 = (bf16[2,512,640]{2,1,0:T(8,128)(2,1)}, bf16[2,512,640]{2,1,0:T(8,128)(2,1)S(1)}, u32[]{:S(2)}) copy-start(bf16[2,512,640]{2,1,0:T(8,128)(2,1)S(1)} %pad_maximum_fusion.1) | copy-start | bytes 3932164
  115.6 6.4 %collective-permute-start.21 = (f32[2,640]{1,0:T(2,128)S(1)}, f32[2,640]{1,0:T(2,128)S(1)}, u32[]{:S(2)}, u32[]{:S(2)}) collective-permute-start(f32[2,640]{1,0:T(2,128)S(1)} %add.77), channel_id=1, source_target_pairs={{0,16},{4,20},{8,24},{12,28},{16,0},{20,4},{24,8},{28,12},{32,48},... | collective-permute-start | bytes 15368 | tf_op jit(solution)/shard_map/ppermute | solution.py:46
  117.7 4.4 %collective-permute-start.22 = (f32[2,640]{1,0:T(2,128)S(1)}, f32[2,640]{1,0:T(2,128)S(1)}, u32[]{:S(2)}, u32[]{:S(2)}) collective-permute-start(f32[2,640]{1,0:T(2,128)S(1)} %add.77), channel_id=1, source_target_pairs={{0,24},{4,28},{8,0},{12,4},{16,8},{20,12},{24,16},{28,20},{32,56},... | collective-permute-start | bytes 15368 | tf_op jit(solution)/shard_map/ppermute | solution.py:46
  119.5 2.0 %copy-start.5 = (bf16[512,640]{1,0:T(8,128)(2,1)S(1)}, bf16[512,640]{1,0:T(8,128)(2,1)}, u32[]{:S(2)}) copy-start(bf16[512,640]{1,0:T(8,128)(2,1)} %param.8) | copy-start | bytes 1966084
  119.7 8.0 %collective-permute-start.24 = (bf16[2,512,128]{2,1,0:T(8,128)(2,1)S(1)}, bf16[2,512,128]{2,1,0:T(8,128)(2,1)S(1)}, u32[]{:S(2)}, u32[]{:S(2)}) collective-permute-start(bf16[2,512,128]{2,1,0:T(8,128)(2,1)S(1)} %get-tuple-element.107), channel_id=1, source_target_pairs={{0,4},{4,0},{8,12},{12,8},{16,20},{20,16},{24,28},{28,24},{32,36},... | collective-permute-start | bytes 786440 | tf_op jit(solution)/shard_map/ppermute | solution.py:36
  127.7 16.4 %collective-permute-start.26 = (f32[2,640]{1,0:T(2,128)S(1)}, f32[2,640]{1,0:T(2,128)S(1)}, u32[]{:S(2)}, u32[]{:S(2)}) collective-permute-start(f32[2,640]{1,0:T(2,128)S(1)} %add_add_fusion.2), channel_id=1, source_target_pairs={{0,32},{4,36},{8,40},{12,44},{16,48},{20,52},{24,56},{28,60},{32,6... | collective-permute-start | bytes 15368 | tf_op jit(solution)/shard_map/ppermute | solution.py:46
  129.6 14.4 %collective-permute-start.27 = (f32[2,640]{1,0:T(2,128)S(1)}, f32[2,640]{1,0:T(2,128)S(1)}, u32[]{:S(2)}, u32[]{:S(2)}) collective-permute-start(f32[2,640]{1,0:T(2,128)S(1)} %add_add_fusion.2), channel_id=1, source_target_pairs={{0,64},{4,68},{8,72},{12,76},{16,80},{20,84},{24,88},{28,92},{32,9... | collective-permute-start | bytes 15368 | tf_op jit(solution)/shard_map/ppermute | solution.py:46
  131.3 12.8 %collective-permute-start.28 = (f32[2,640]{1,0:T(2,128)S(1)}, f32[2,640]{1,0:T(2,128)S(1)}, u32[]{:S(2)}, u32[]{:S(2)}) collective-permute-start(f32[2,640]{1,0:T(2,128)S(1)} %add_add_fusion.2), channel_id=1, source_target_pairs={{0,96},{4,100},{8,104},{12,108},{16,112},{20,116},{24,120},{28,124... | collective-permute-start | bytes 15368 | tf_op jit(solution)/shard_map/ppermute | solution.py:46
  133.0 1.1 copy-start.3
  140.2 1.2 copy-start.6
  140.2 1.8 %copy-start.8 = (bf16[2,512,640]{2,1,0:T(8,128)(2,1)S(1)}, bf16[2,512,640]{2,1,0:T(8,128)(2,1)}, u32[]{:S(2)}) copy-start(bf16[2,512,640]{2,1,0:T(8,128)(2,1)} %copy-done.7) | copy-start | bytes 3932164
